TPU v7x, 512 devices: a whole 4x8x8 slice. The times are simulated.
512 devices in a mesh: ja: 64 (over z, x, core), aa: 8 (over y).
Axes of the slice: x: 4, y: 8, z: 8, core: 2. Of those that a mesh axis runs over, the one named last changes fastest.
Arguments:
- state: float32 [12, 131072], P(None, 'ja'), may hold values from -6 to 6
- mass: float32 [131072], P('ja'), may hold values from 0.2 to 5
- levels: int32 [131072], P('ja'), may hold values from 0 to 5, as said below
- ticks: int32 [131072], P('ja'), may hold values from 0 to 32, as said below
- active: int32 [10240], replicated, may hold values from 0 to 131071, as said below
Outputs:
- new_active: float32 [12, 10240], P(None, 'aa')
- new_state: float32 [12, 131072], P(None, 'ja')
Inputs may be any that keep to these rules, and one draw needn't show every extreme that they name: `levels`: a star's step is 0.25 * 2**(-level). `ticks`: below 2**(5 - levels) for a star not in active, equal to 2**(5 - levels) for a star in active. Distinct star indices; entries b * 1280 to (b + 1) * 1280 - 1 form active block b.
All inputs are finite; a program needn't handle non-finite values.
Results may differ from a plain program's by a relative error of at most 0.0003.
Values sent between devices are 32-bit elements; how exact they have to be, the bound alone decides.
No kernel may reach another device: no remote copies, remote signals or barrier semaphores. Data moves between devices by JAX's collectives and lax.ppermute only.
A program may use at most 64 MiB of HBM per device.

v0:
```python
import jax
import jax.numpy as jnp
from jax import lax
from jax.sharding import PartitionSpec as P

LEVELS = 5


EPS2 = 0.0001
H_MAX = 0.25


def predict(state, ticks):
    dt = ticks.astype(jnp.float32) * (H_MAX / 2**LEVELS)
    pos, vel, acc, jerk = (state[0:3], state[3:6], state[6:9], state[9:12])
    predicted = pos + dt * (vel + dt * (0.5 * acc + dt * (jerk / 6.0)))
    predicted_vel = vel + dt * (acc + dt * (0.5 * jerk))
    return (predicted, predicted_vel)


def field_terms(targets, predicted, predicted_vel, mass):
    dx = predicted[0][None, :] - targets[0][:, None]
    dy = predicted[1][None, :] - targets[1][:, None]
    dz = predicted[2][None, :] - targets[2][:, None]
    wx = predicted_vel[0][None, :] - targets[3][:, None]
    wy = predicted_vel[1][None, :] - targets[4][:, None]
    wz = predicted_vel[2][None, :] - targets[5][:, None]
    total = dx * dx + dy * dy + dz * dz + EPS2
    inverse = lax.rsqrt(total)
    weight = mass[None, :] * inverse * inverse * inverse
    rate = 3.0 * (dx * wx + dy * wy + dz * wz) / total
    return jnp.stack(
        [
            jnp.sum(weight * dx, axis=1),
            jnp.sum(weight * dy, axis=1),
            jnp.sum(weight * dz, axis=1),
            jnp.sum(weight * (wx - rate * dx), axis=1),
            jnp.sum(weight * (wy - rate * dy), axis=1),
            jnp.sum(weight * (wz - rate * dz), axis=1),
        ]
    )


def correct(states, step, forces):
    pos, vel, old_acc, old_jerk = (states[0:3], states[3:6], states[6:9], states[9:12])
    acc_new, jerk_new = (forces[0:3], forces[3:6])
    error = old_acc - acc_new
    second = -6.0 * error - step * (4.0 * old_jerk + 2.0 * jerk_new)
    third = 12.0 * error + 6.0 * step * (old_jerk + jerk_new)
    fixed_pos = pos + step * step * (second / 24.0 + third / 120.0)
    fixed_vel = vel + step * (second / 6.0 + third / 24.0)
    return jnp.concatenate([fixed_pos, fixed_vel, acc_new, jerk_new], axis=0)


def per_device(state, mass, levels, ticks, active):
    j_dev = state.shape[1]
    ja_count = lax.axis_size("ja")
    aa_count = lax.axis_size("aa")
    start = lax.axis_index("ja") * j_dev
    predicted, predicted_vel = predict(state, ticks)
    step_all = H_MAX * jnp.exp2(-levels.astype(jnp.float32))
    table = jnp.concatenate([predicted, predicted_vel, state[6:12], step_all[None, :]], axis=0)
    a_dev = active.shape[0] // aa_count
    mine = lax.dynamic_slice_in_dim(active, lax.axis_index("aa") * a_dev, a_dev)
    local = mine - start
    inside = ((local >= 0) & (local < j_dev)).astype(jnp.float32)
    picked = jnp.take(table, jnp.clip(local, 0, j_dev - 1), axis=1) * inside[None, :]
    assembled = lax.psum(picked, "ja")
    blocks = assembled[0:6].reshape(6, a_dev // 64, 64).transpose(1, 0, 2)
    terms = lax.map(lambda targets: field_terms(targets, predicted, predicted_vel, mass), blocks)
    partial_value = terms.transpose(1, 0, 2).reshape(6, a_dev)
    scale = 1.0 / (j_dev * ja_count)
    forces = lax.psum(partial_value, "ja") * scale
    new_active = correct(assembled[0:12], assembled[12], forces)
    updates = lax.all_gather(new_active, "aa", axis=1, tiled=True)
    target = active - start
    target = jnp.where((target >= 0) & (target < j_dev), target, j_dev)
    new_state = state.at[:, target].set(updates, mode="drop")
    return (new_active, new_state)


def solution(mesh):
    return jax.shard_map(
        per_device,
        mesh=mesh,
        in_specs=(P(None, "ja"), P("ja"), P("ja"), P("ja"), P()),
        out_specs=(P(None, "aa"), P(None, "ja")),
        check_vma=False,
    )
```

profile of v0, /device:TPU:1, one launch (start us, length us, event | category | flops | bytes accessed | tf_op | source)
XLA Modules:
  0.0 529.0 jit_solution(1504297755358503834)
XLA Ops:
  7.2 0.0 all-reduce.2.cloned.1.call-start
  7.2 0.7 exponential_multiply_fusion
  7.9 0.8 compare_and_fusion
  8.7 0.7 convert_multiply_fusion
  9.4 0.9 slice.91
  10.4 1.0 multiply_add_fusion
  11.4 0.4 copy.72
  11.8 2.4 gather_fusion
  14.2 0.2 copy.73
  14.4 0.7 multiply_bitcast_fusion
  15.1 0.0 all-reduce.2.cloned.1.call-update
  15.1 0.8 compare_select_fusion
  15.9 1.3 copy.76
  17.2 184.3 %all-reduce.2.cloned.1.call-done = f32[13,1280]{1,0:T(8,128)} async-done(((f32[13,1280]{1,0:T(8,128)}), f32[13,1280]{1,0:T(8,128)}) %all-reduce.2.cloned.1.call-update) | async-done | bytes 66576 | tf_op jit(solution)/shard_map/psum | solution.py:68
  201.5 0.8 slice.105
  202.3 0.1 reshape.36
  202.4 0.0 copy-done.1
  202.4 22.9 %while.10 = (s32[]{:T(128)}, f32[20,6,64]{2,1,0:T(8,128)S(1)}, f32[2048]{0:T(1024)S(1)}, f32[3,2048]{1,0:T(4,128)S(1)}, f32[20,6,64]{2,1,0:T(8,128)S(1)}, /*index=5*/f32[3,2048]{1,0:T(4,128)S(1)}, s32[]{:T(128)}) while((s32[]{:T(128)}, f32[20,6,64]{2,1,0:T(8,128)S(1)}, f32[2048]{0:T(1024)S(1)}, f32[3,2048]{1,0:T(4,128)S(1)}, ...), condition=%wide.region_8.9_spmd, body=%wide.region_1.8_spmd.sunk | while | flops 5242498 | bytes 176221 | solution.py:70
  202.5 1.0 fusion.21
  203.6 1.0 fusion.21
  204.8 1.0 fusion.21
  205.9 1.0 fusion.21
  207.1 1.0 fusion.21
  208.2 1.0 fusion.21
  209.4 1.0 fusion.21
  210.5 1.0 fusion.21
  211.7 1.0 fusion.21
  212.8 1.0 fusion.21
  213.9 1.0 fusion.21
  215.1 1.0 fusion.21
  216.2 1.0 fusion.21
  217.4 1.0 fusion.21
  218.5 1.0 fusion.21
  219.7 1.0 fusion.21
  220.8 1.0 fusion.21
  222.0 1.0 fusion.21
  223.1 1.0 fusion.21
  224.3 1.0 fusion.21
  225.4 0.1 reshape.37
  225.4 242.6 %psum.15 = f32[6,1280]{1,0:T(8,128)S(1)} all-reduce(f32[6,1280]{1,0:T(8,128)S(1)} %reshape.37), channel_id=1, replica_groups=mesh['ja'=64,'aa'=8] {'ja'}, use_global_device_ids=true, to_apply=%region_9.10 | all-reduce | flops 7680 | bytes 61440 | tf_op jit(solution)/shard_map/psum | solution.py:73
  468.1 0.8 multiply_reduce_fusion.1
  468.9 0.9 slice_add_fusion.1
  469.8 0.8 slice_add_fusion
  470.7 0.0 copy-start
  470.7 21.2 %all_gather.3 = f32[12,10240]{1,0:T(8,128)S(1)} all-gather(f32[12,1280]{1,0:T(8,128)S(1)} %pad_maximum_fusion.1), channel_id=1, replica_groups=mesh['ja'=64,'aa'=8] {'aa'}, dimensions={1}, use_global_device_ids=true | all-gather | bytes 552960 | tf_op jit(solution)/shard_map/all_gather | solution.py:75
  491.9 3.1 copy.77
  495.0 26.2 %scatter_fusion = f32[12,2048]{0,1:T(8,128)S(1)} fusion(f32[12,2048]{0,1:T(8,128)S(1)} %copy.76, s32[10240]{0:T(1024)S(1)} %compare_select_fusion, f32[10240,12]{1,0:T(8,128)} %copy.77), kind=kCustom, calls=%fused_computation.1 | custom fusion | bytes 1515520 | tf_op jit(solution)/shard_map/scatter | solution.py:78
  521.2 1.0 copy.78
  (109 shorter events, 1.8 us)
Async XLA Ops:
  7.2 195.2 %copy-start.1 = (f32[2048]{0:T(1024)S(1)}, f32[2048]{0:T(1024)}, u32[]{:S(2)}) copy-start(f32[2048]{0:T(1024)} %param.8) | copy-start | bytes 24580
  7.2 194.3 %all-reduce.2.cloned.1.call-start = ((), (), s32[]{:S(2)}) async-start(), calls=%async_computation | async-start | bytes 163840 | tf_op jit(solution)/shard_map/psum | solution.py:68
  470.7 50.5 %copy-start = (f32[12,1280]{1,0:T(8,128)}, f32[12,1280]{1,0:T(8,128)S(1)}, u32[]{:S(2)}) copy-start(f32[12,1280]{1,0:T(8,128)S(1)} %pad_maximum_fusion.1) | copy-start | bytes 184324
Sparse Core Ops, SparseCore 0:
  15.2 186.2 all-reduce.1
where the time goes:
time: 539 us; the launch traced here: 529 us
  blocking collectives  264 us (49%)
  waiting for transfers between devices  184 us (34%)
  local copies, waits for them, and re-layouts  38.1 us (7%)
  other arithmetic  27.6 us (5%)
  between operations  14.2 us (3%)
    psum x1, blocking collectives, per_device(): forces = lax.psum(partial_value, 'ja') * scale  243 us
    psum x1, waiting for transfers between devices, per_device(): assembled = lax.psum(picked, 'ja')  184 us
    scatter x1, local copies, waits for them, and re-layouts, per_device(): new_state = state.at[:, target].set(updates, mode='drop')  26.2 us
    all_gather x1, blocking collectives, per_device(): updates = lax.all_gather(new_active, 'aa', axis=1, tiled=True)  21.2 us
    reduce_sum x20, other arithmetic, field_terms(): jnp.sum(weight * (wz - rate * dz), axis=1)  20.3 us
  transfers between devices with their start and end apart: 1, of which 1 were waited for; matrix products, arithmetic and copies ran while one was open for 0% of the time, Pallas kernels for 0%

commit v1 on v0

v1 whole, which is shorter than its diff:
```python
import jax
import jax.numpy as jnp
from jax import lax
from jax.experimental import pallas as pl
from jax.experimental.pallas import tpu as pltpu
from jax.sharding import Mesh, PartitionSpec as P

LEVELS = 5
EPS2 = 0.0001
H_MAX = 0.25
TICK = H_MAX / 2**LEVELS

X, C = 4, 2
GROUPS = X * C
TILES = 16
MAIN, TAIL = 128, 32
PER = MAIN + TAIL
FIELD = 8 * TILES
CHUNK = 512

f32, bf16 = jnp.float32, jnp.bfloat16


def params():
    return pltpu.CompilerParams(vmem_limit_bytes=48 * 1024 * 1024)


def vmem(n):
    return [pl.BlockSpec(memory_space=pltpu.VMEM)] * n


def predict(pos, vel, acc, jerk, dt):
    predicted = pos + dt * (vel + dt * (0.5 * acc + dt * (jerk / 6.0)))
    predicted_vel = vel + dt * (acc + dt * (0.5 * jerk))
    return predicted, predicted_vel


def step_of(levels):
    return jnp.left_shift(jnp.ones_like(levels), LEVELS - levels).astype(f32) * TICK


def correct(pos, vel, old_acc, old_jerk, step, acc_new, jerk_new):
    error = old_acc - acc_new
    second = -6.0 * error - step * (4.0 * old_jerk + 2.0 * jerk_new)
    third = 12.0 * error + 6.0 * step * (old_jerk + jerk_new)
    fixed_pos = pos + step * step * (second / 24.0 + third / 120.0)
    fixed_vel = vel + step * (second / 6.0 + third / 24.0)
    return fixed_pos, fixed_vel


def split3(value):
    first = value.astype(bf16)
    rest = value - first.astype(f32)
    second = rest.astype(bf16)
    return first, second, (rest - second.astype(f32)).astype(bf16)


def pack(main, tail, spare=None):
    if spare is None:
        spare = jnp.zeros((1, TAIL), f32)
    last = jnp.concatenate([tail[0:1], tail[1:2], tail[2:3], spare], axis=1)
    return jnp.concatenate([main, last], axis=0)


def first_star():
    return ((lax.axis_index("z") * X + lax.axis_index("x")) * C + lax.axis_index("c")) * (TILES * 128)


def pick_kernel(state_ref, mass_ref, ticks_ref, levels_ref, active_ref, msg_ref, table_ref):
    start = first_star()
    block = lax.axis_index("aa") * 10
    zero = jnp.zeros((1, 128), f32)
    for i in range(TILES):
        s = state_ref[:, i * 128 : (i + 1) * 128]
        dt = ticks_ref[i : i + 1, :].astype(f32) * TICK
        pos, vel = predict(s[0:3], s[3:6], s[6:9], s[9:12], dt)
        step = step_of(levels_ref[i : i + 1, :])
        field = jnp.concatenate([pos, vel, mass_ref[i : i + 1, :], zero], axis=0)
        both = jnp.concatenate([field, s[6:12], step, zero], axis=0)
        for n, part in enumerate(split3(both)):
            table_ref[n * 256 + i * 16 : n * 256 + (i + 1) * 16, :] = part
        for g in range(GROUPS):
            msg_ref[g, i * 8 : (i + 1) * 8, :] = field
    rows = lax.broadcasted_iota(jnp.int32, (128, 128), 0)
    picks = []
    for k in range(10):
        local = active_ref[pl.ds(block + k, 1), :] - start
        high = jnp.broadcast_to(jnp.right_shift(local, 7), (16, 128))
        low = jnp.bitwise_and(local, 127)
        chosen = jnp.where(rows == low, 1.0, 0.0).astype(bf16)
        found = jnp.dot(table_ref[...], chosen, preferred_element_type=f32)
        pick = jnp.zeros((16, 128), f32)
        for h in range(TILES):
            r = slice(h * 16, (h + 1) * 16)
            value = (found[0:256][r] + found[256:512][r]) + found[512:768][r]
            pick = jnp.where(high == h, value, pick)
        picks.append(pick)
    for g in range(GROUPS):
        main = picks[g]
        tail = picks[8 + g // 4][:, (g % 4) * TAIL : (g % 4 + 1) * TAIL]
        msg_ref[g, FIELD : FIELD + 4, :] = pack(main[0:3], tail[0:3])
        msg_ref[g, FIELD + 4 : FIELD + 8, :] = pack(main[3:6], tail[3:6])
        msg_ref[g, FIELD + 8 : FIELD + 12, :] = pack(main[8:11], tail[8:11], tail[14:15])
        msg_ref[g, FIELD + 12 : FIELD + 16, :] = pack(main[11:14], tail[11:14])
        msg_ref[g, 7:8, :] = main[14:15]


def sum_kernel(got_ref, first_ref, out_ref, keep_ref):
    total = got_ref[0]
    step = first_ref[0]
    for g in range(1, GROUPS):
        total = total + got_ref[g]
        step = step + first_ref[g]
    for z in range(out_ref.shape[0]):
        out_ref[z] = total[0:8]
    keep_ref[0:8, :] = total[8:16]
    keep_ref[8:16, :] = step


def force_kernel(targets_ref, got_ref, keep_ref, out_ref, seen_ref, weight_ref, left0_ref, left1_ref, sums_ref):
    target = targets_ref[0]
    for z in range(1, targets_ref.shape[0]):
        target = target + targets_ref[z]
    columns = jnp.transpose(target)
    for half in range(2):
        for q in range(3):
            seen_ref[half * 3 + q, 0:MAIN, :] = jnp.broadcast_to(columns[:, half * 4 + q : half * 4 + q + 1], (MAIN, 128))
            seen_ref[half * 3 + q, MAIN:PER, :] = jnp.broadcast_to(
                columns[q * TAIL : (q + 1) * TAIL, half * 4 + 3 : half * 4 + 4], (TAIL, 128)
            )

    row = lax.broadcasted_iota(jnp.int32, (8, 128), 0)

    def weigh(g, _):
        for i in range(TILES):
            tile = got_ref[g, i * 8 : (i + 1) * 8, :]
            mass = tile[6:7]
            value = jnp.where(row < 6, tile * mass, jnp.where(row == 6, tile, 0.0))
            first = value.astype(bf16).astype(f32)
            rest = value - first
            second = rest.astype(bf16).astype(f32)
            rows = jnp.concatenate([first, second, rest - second, jnp.zeros_like(value)], axis=0).astype(bf16)
            weight_ref[:, pl.ds(pl.multiple_of((g * TILES + i) * 128, 128), 128)] = rows
        return 0

    lax.fori_loop(0, GROUPS, weigh, 0)
    sums_ref[...] = jnp.zeros_like(sums_ref)

    def fill(left_ref, chunk):
        per_group = TILES * 128 // CHUNK
        g, part = chunk // per_group, chunk % per_group
        for j in range(CHUNK // 128):
            base = pl.multiple_of(part * (CHUNK // 16) + j * 8, 8)
            star = [jnp.broadcast_to(got_ref[g, pl.ds(base + q, 1), :], (16, 128)) for q in range(6)]
            for b in range(PER // 16):
                r = slice(b * 16, (b + 1) * 16)
                dx, dy, dz, wx, wy, wz = [star[q] - seen_ref[q, r, :] for q in range(6)]
                total = (dx * dx + EPS2) + dy * dy + dz * dz
                along = dx * wx + dy * wy + dz * wz
                inverse = lax.rsqrt(total)
                square = inverse * inverse
                cube = square * inverse
                rate = cube * (square * along)
                cube_high = cube.astype(bf16)
                cube_low = (cube - cube_high.astype(f32)).astype(bf16)
                rate_high = rate.astype(bf16)
                rate_low = (rate - rate_high.astype(f32)).astype(bf16)
                for n, part_value in enumerate((cube_high, cube_low, rate_high, rate_low)):
                    left_ref[n * PER + b * 16 : n * PER + (b + 1) * 16, j * 128 : (j + 1) * 128] = part_value

    def gather(left_ref, chunk):
        weight = weight_ref[:, pl.ds(pl.multiple_of(chunk * CHUNK, CHUNK), CHUNK)]
        sums_ref[...] += lax.dot_general(left_ref[...], weight, (((1,), (1,)), ((), ())), preferred_element_type=f32)

    chunks = GROUPS * TILES * 128 // CHUNK
    fill(left0_ref, 0)

    def body(n, _):
        fill(left1_ref, 2 * n + 1)
        gather(left0_ref, 2 * n)
        fill(left0_ref, jnp.minimum(2 * n + 2, chunks - 1))
        gather(left1_ref, 2 * n + 1)
        return 0

    lax.fori_loop(0, chunks // 2, body, 0)

    def columns_of(first):
        total = sums_ref[first : first + PER, :] + sums_ref[first + PER : first + 2 * PER, :]
        main = jnp.transpose(total[0:MAIN])
        tail = jnp.transpose(total[MAIN:PER])
        return main[0:8] + main[8:16] + main[16:24], tail[0:8] + tail[8:16] + tail[16:24]

    def three(value):
        return jnp.concatenate([value, value, value], axis=0)

    main, tail = columns_of(0)
    cube_pos = pack(main[0:3], tail[0:3])
    cube_vel = pack(main[3:6], tail[3:6])
    cube_one = pack(three(main[6:7]), three(tail[6:7]))
    main, tail = columns_of(2 * PER)
    rate_pos = pack(main[0:3], tail[0:3])
    rate_one = pack(three(main[6:7]), three(tail[6:7]))
    acc = cube_pos - target[0:4] * cube_one
    jerk = (cube_vel - target[4:8] * cube_one) - 3.0 * (rate_pos - target[0:4] * rate_one)
    forces = jnp.concatenate([acc, jerk], axis=0)
    for z in range(out_ref.shape[0]):
        out_ref[z, 0:8, :] = forces
        out_ref[z, 8:24, :] = keep_ref[...]


def correct_kernel(scale, targets_ref, got_ref, out_ref):
    target = targets_ref[0]
    total = got_ref[0]
    for z in range(1, targets_ref.shape[0]):
        target = target + targets_ref[z]
        total = total + got_ref[z]
    forces = total[0:8] * scale
    old = total[8:16]
    main = total[23:24]
    tail = old[3:4, 96:128]
    step = pack(jnp.concatenate([main, main, main], axis=0), jnp.concatenate([tail, tail, tail], axis=0))
    pos, vel = correct(target[0:4], target[4:8], old[0:4], old[4:8], step, forces[0:4], forces[4:8])
    both = jnp.concatenate([pos, vel], axis=0)
    for d in range(out_ref.shape[0]):
        out_ref[d, 0:8, :] = forces
        out_ref[d, 8:16, :] = both


def store_kernel(state_ref, ticks_ref, levels_ref, active_ref, got_ref, new_active_ref, new_state_ref, left_ref, low_ref, sums_ref):
    start = first_star()
    mine = lax.axis_index("aa")

    def tails(c, y, row):
        parts = [got_ref[c, y * X + x, row : row + 1, :] for x in range(X)]
        return jnp.concatenate(
            [jnp.concatenate([p[:, q * TAIL : (q + 1) * TAIL] for p in parts], axis=1) for q in range(3)], axis=0
        )

    for c in range(C):
        for x in range(X):
            lanes = slice((c * X + x) * 128, (c * X + x + 1) * 128)
            tile = got_ref[c, mine * X + x]
            new_active_ref[0:3, lanes] = tile[8:11]
            new_active_ref[3:6, lanes] = tile[12:15]
            new_active_ref[6:9, lanes] = tile[0:3]
            new_active_ref[9:12, lanes] = tile[4:7]
        lanes = slice(1024 + c * 128, 1024 + (c + 1) * 128)
        new_active_ref[0:3, lanes] = tails(c, mine, 11)
        new_active_ref[3:6, lanes] = tails(c, mine, 15)
        new_active_ref[6:9, lanes] = tails(c, mine, 3)
        new_active_ref[9:12, lanes] = tails(c, mine, 7)

    row8 = lax.broadcasted_iota(jnp.int32, (8, 128), 0)
    rows = lax.broadcasted_iota(jnp.int32, (128, 128), 0)
    one = jnp.ones((1, 128), f32)
    sums_ref[...] = jnp.zeros_like(sums_ref)

    def block(y, _):
        def put(k, value):
            local = active_ref[pl.ds(y * 10 + k, 1), :] - start
            high = jnp.broadcast_to(jnp.right_shift(local, 7), (16, 128))
            low = jnp.bitwise_and(local, 127)
            lanes = slice(k * 128, (k + 1) * 128)
            low_ref[:, lanes] = jnp.where(rows == low, 1.0, 0.0).astype(bf16)
            first = value.astype(bf16).astype(f32)
            both = jnp.concatenate([first, value - first], axis=0)
            for h in range(TILES):
                left_ref[h * 16 : (h + 1) * 16, lanes] = jnp.where(high == h, both, 0.0).astype(bf16)

        for c in range(C):
            for x in range(X):
                put(c * X + x, jnp.where(row8 == 3, 1.0, got_ref[c, y * X + x, 0:8, :]))
            put(8 + c, jnp.concatenate([tails(c, y, 3), one, tails(c, y, 7), one], axis=0))
        sums_ref[...] += lax.dot_general(
            left_ref[...], low_ref[...], (((1,), (1,)), ((), ())), preferred_element_type=f32
        )
        return 0

    lax.fori_loop(0, got_ref.shape[1] // X, block, 0)

    for i in range(TILES):
        lanes = slice(i * 128, (i + 1) * 128)
        s = state_ref[:, lanes]
        forces = sums_ref[i * 16 : i * 16 + 8, :] + sums_ref[i * 16 + 8 : i * 16 + 16, :]
        acc, jerk, hit = forces[0:3], forces[4:7], forces[3:4] > 0.5
        dt = ticks_ref[i : i + 1, :].astype(f32) * TICK
        step = step_of(levels_ref[i : i + 1, :])
        pos, vel = predict(s[0:3], s[3:6], s[6:9], s[9:12], dt)
        pos, vel = correct(pos, vel, s[6:9], s[9:12], step, acc, jerk)
        new = jnp.concatenate([pos, vel, acc, jerk], axis=0)
        new_state_ref[:, lanes] = jnp.where(hit, new, s)


def per_device(state, mass, levels, ticks, active):
    z_count, y_count = lax.axis_size("z"), lax.axis_size("aa")
    n_stars = state.shape[1] * z_count * GROUPS
    mass, levels, ticks = [a.reshape(TILES, 128) for a in (mass, levels, ticks)]
    active = active.reshape(-1, 128)

    message = pl.pallas_call(
        pick_kernel,
        out_shape=jax.ShapeDtypeStruct((GROUPS, FIELD + 16, 128), f32),
        in_specs=vmem(5),
        out_specs=vmem(1)[0],
        scratch_shapes=[pltpu.VMEM((768, 128), bf16)],
        compiler_params=params(),
    )(state, mass, ticks, levels, active)
    got = lax.all_to_all(message, ("c", "x"), 0, 0, tiled=True)

    targets, keep = pl.pallas_call(
        sum_kernel,
        grid=(1,),
        out_shape=[jax.ShapeDtypeStruct((z_count, 8, 128), f32), jax.ShapeDtypeStruct((16, 128), f32)],
        in_specs=[
            pl.BlockSpec((GROUPS, 16, 128), lambda i: (0, FIELD // 16, 0)),
            pl.BlockSpec((GROUPS, 8, 128), lambda i: (0, 0, 0)),
        ],
        out_specs=[pl.BlockSpec((z_count, 8, 128), lambda i: (0, 0, 0)), pl.BlockSpec((16, 128), lambda i: (0, 0))],
        compiler_params=params(),
    )(got, got)
    targets = lax.all_to_all(targets, "z", 0, 0, tiled=True)

    partial = pl.pallas_call(
        force_kernel,
        out_shape=jax.ShapeDtypeStruct((z_count, 24, 128), f32),
        in_specs=vmem(3),
        out_specs=vmem(1)[0],
        scratch_shapes=[
            pltpu.VMEM((6, PER, 128), f32),
            pltpu.VMEM((32, GROUPS * TILES * 128), bf16),
            pltpu.VMEM((4 * PER, CHUNK), bf16),
            pltpu.VMEM((4 * PER, CHUNK), bf16),
            pltpu.VMEM((4 * PER, 32), f32),
        ],
        compiler_params=params(),
    )(targets, got, keep)
    partial = lax.all_to_all(partial, "z", 0, 0, tiled=True)

    updates = pl.pallas_call(
        lambda *refs: correct_kernel(1.0 / n_stars, *refs),
        out_shape=jax.ShapeDtypeStruct((y_count * X, 16, 128), f32),
        in_specs=vmem(2),
        out_specs=vmem(1)[0],
        compiler_params=params(),
    )(targets, partial)
    updates = lax.all_to_all(updates, ("aa", "x"), 0, 0, tiled=True)
    updates = lax.all_gather(updates, "c")

    new_active, new_state = pl.pallas_call(
        store_kernel,
        out_shape=[jax.ShapeDtypeStruct((12, 1280), f32), jax.ShapeDtypeStruct(state.shape, f32)],
        in_specs=vmem(5),
        out_specs=vmem(2),
        scratch_shapes=[
            pltpu.VMEM((256, 1280), bf16),
            pltpu.VMEM((128, 1280), bf16),
            pltpu.VMEM((256, 128), f32),
        ],
        compiler_params=params(),
    )(state, ticks, levels, active, updates)
    return new_active, new_state


def solution(mesh):
    shape = (mesh.shape["ja"] // GROUPS, X, C, mesh.shape["aa"])
    fine = Mesh(mesh.devices.reshape(shape), ("z", "x", "c", "aa"))
    ja = ("z", "x", "c")
    return jax.shard_map(
        per_device,
        mesh=fine,
        in_specs=(P(None, ja), P(ja), P(ja), P(ja), P()),
        out_specs=(P(None, "aa"), P(None, ja)),
        check_vma=False,
    )
```

time: 539 us -> 95.8 us (0.18); the launches traced: 529 us -> 95.4 us
  blocking collectives: 264 us -> 67.3 us
  waiting for transfers between devices: 184 us -> 0 us
  local copies, waits for them, and re-layouts: 38.1 us -> 3.78 us
  other arithmetic: 27.6 us -> 0 us
  Pallas kernels: 0 us -> 23.7 us
  between operations: 14.2 us -> 0.68 us
    psum x1 -> x0, blocking collectives: 243 us -> none  [per_device(): forces = lax.psum(partial_value, 'ja') * scale]
    psum x1 -> x0, waiting for transfers between devices: 184 us -> none  [per_device(): assembled = lax.psum(picked, 'ja')]
    all_to_all x0 -> x4, blocking collectives: none -> 60.8 us  [the longest x1 19.6 us: per_device(): got = lax.all_to_all(message, ('c', 'x'), 0, 0, tiled=True)]
    scatter x1 -> x0, local copies, waits for them, and re-layouts: 26.2 us -> none  [per_device(): new_state = state.at[:, target].set(updates, mode='drop')]
    pallas_call x0 -> x5, Pallas kernels: none -> 23.7 us  [the longest x1 18.3 us: per_device(): pl.pallas_call(force_kernel, out_shape=jax.ShapeDtypeStruct((z_count, 24,...]
    reduce_sum x20 -> x0, other arithmetic: 20.3 us -> none  [field_terms(): jnp.sum(weight * (wz - rate * dz), axis=1)]
    all_gather x1, blocking collectives: 21.2 us -> 6.49 us  [per_device(): updates = lax.all_gather(updates, 'c')]
  transfers between devices with their start and end apart: 1 -> 0, of which waited for: 1 -> 0; matrix products, arithmetic and copies ran while one was open for 0% -> 0% of each run, Pallas kernels for 0% -> 0%
where the time goes in v1:
time: 95.8 us; the launch traced here: 95.4 us
  blocking collectives  67.3 us (70%)
  Pallas kernels  23.7 us (25%)
  local copies, waits for them, and re-layouts  3.78 us (4%)
    all_to_all x1, blocking collectives, per_device(): got = lax.all_to_all(message, ('c', 'x'), 0, 0, tiled=True)  19.6 us
    pallas_call x1, Pallas kernels, per_device(): pl.pallas_call(force_kernel, out_shape=jax.ShapeDtypeStruct((z_count, 24,...  18.3 us
    all_to_all x1, blocking collectives, per_device(): updates = lax.all_to_all(updates, ('aa', 'x'), 0, 0, tiled=True)  18 us
    all_to_all x1, blocking collectives, per_device(): targets = lax.all_to_all(targets, 'z', 0, 0, tiled=True)  13.2 us
    all_to_all x1, blocking collectives, per_device(): partial = lax.all_to_all(partial, 'z', 0, 0, tiled=True)  9.96 us
    all_gather x1, blocking collectives, per_device(): updates = lax.all_gather(updates, 'c')  6.49 us
    pallas_call x1, Pallas kernels, per_device(): pl.pallas_call(store_kernel, out_shape=[jax.ShapeDtypeStruct((12, 1280),...  4.37 us
    unnamed x18, local copies, waits for them, and re-layouts  3.78 us

profile of v1, /device:TPU:1, one launch (start us, length us, event | category | flops | bytes accessed | tf_op | source)
XLA Modules:
  0.0 95.4 jit_solution(10051001280364869956)
XLA Ops:
  0.6 0.0 copy-start
  0.6 0.9 copy-done
  1.5 0.0 copy-start.2
  1.5 0.8 copy-done.2
  2.3 0.0 copy-start.4
  2.3 0.7 copy-done.4
  3.0 0.0 copy-start.6
  3.0 0.7 copy-done.6
  3.7 0.0 copy-start.8
  3.7 0.7 copy-done.8
  4.4 0.9 shard_map.68
  5.3 19.6 %all_to_all.20.got_ref.first_ref = f32[8,144,128]{2,1,0:T(8,128)S(1)} all-to-all(f32[8,144,128]{2,1,0:T(8,128)S(1)} %shard_map.68), channel_id=1, replica_groups=mesh['z'=8,'x'=4,'c'=2,'aa'=8] {'c','x'}, dimensions={0} | all-to-all | bytes 1179648 | tf_op jit(solution)/shard_map/all_to_all | solution.py:308
  24.9 13.2 %all_to_all.21.targets_ref.refs_0_ = f32[8,8,128]{2,1,0:T(8,128)S(1)} all-to-all(f32[8,8,128]{2,1,0:T(8,128)S(1)} %get-tuple-element.4), channel_id=1, replica_groups=mesh['z'=8,'x'=4,'c'=2,'aa'=8] {'z'}, dimensions={0} | all-to-all | bytes 65536 | tf_op jit(solution)/shard_map/all_to_all | solution.py:321
  38.1 18.3 %shard_map.70 = f32[8,24,128]{2,1,0:T(8,128)S(1)} custom-call(f32[8,8,128]{2,1,0:T(8,128)S(1)} %all_to_all.21.targets_ref.refs_0_, f32[8,144,128]{2,1,0:T(8,128)S(1)} %all_to_all.20.got_ref.first_ref, f32[16,128]{1,0:T(8,128)S(1)} %get-tuple-element.5.keep_ref), custom_call_target="tpu_custom_call" | custom-call | tf_op jit(solution)/shard_map/pallas_call | solution.py:323
  56.4 10.0 %all_to_all.22.refs_1_ = f32[8,24,128]{2,1,0:T(8,128)S(1)} all-to-all(f32[8,24,128]{2,1,0:T(8,128)S(1)} %shard_map.70), channel_id=1, replica_groups=mesh['z'=8,'x'=4,'c'=2,'aa'=8] {'z'}, dimensions={0} | all-to-all | bytes 196608 | tf_op jit(solution)/shard_map/all_to_all | solution.py:337
  66.4 0.1 shard_map.71
  66.5 18.0 %all_to_all.23 = f32[32,16,128]{2,1,0:T(8,128)S(1)} all-to-all(f32[32,16,128]{2,1,0:T(8,128)S(1)} %shard_map.71), channel_id=1, replica_groups=mesh['z'=8,'x'=4,'c'=2,'aa'=8] {'aa','x'}, dimensions={0} | all-to-all | bytes 524288 | tf_op jit(solution)/shard_map/all_to_all | solution.py:346
  84.5 0.0 copy-start.1
  84.5 0.0 copy-start.3
  84.5 0.0 copy-start.5
  84.5 0.0 copy-start.7
  84.5 6.5 %all-gather = f32[64,16,128]{2,1,0:T(8,128)S(1)} all-gather(f32[32,16,128]{2,1,0:T(8,128)S(1)} %all_to_all.23), channel_id=2, replica_groups=mesh['z'=8,'x'=4,'c'=2,'aa'=8] {'c'}, dimensions={0}, use_global_device_ids=true | all-gather | bytes 786432 | tf_op jit(solution)/shard_map/all_gather | solution.py:347
  91.0 0.0 copy-done.1
  91.0 0.0 copy-done.3
  91.0 0.0 copy-done.5
  91.0 0.0 copy-done.7
  91.0 4.4 %shard_map.72 = (f32[12,1280]{1,0:T(8,128)}, f32[12,2048]{1,0:T(8,128)}) custom-call(f32[12,2048]{1,0:T(8,128)S(1)} %copy-done.1, s32[16,128]{1,0:T(8,128)S(1)} %bitcast.9, s32[16,128]{1,0:T(8,128)S(1)} %bitcast.11, s32[80,128]{1,0:T(8,128)S(1)} %bitcast.7, f32[2,32,16,128]{3,2,1,0:T(8,128)S(1)} %bitcast.5), custom_call_target="tpu_custom_call" | custom-call | tf_op jit(solution)/shard_map/pallas_call | solution.py:349
  (1 shorter events, 0.0 us)
Async XLA Ops:
  0.6 0.9 copy-start
  1.5 0.8 copy-start.2
  2.3 0.7 copy-start.4
  3.0 0.7 copy-start.6
  3.7 0.7 copy-start.8
  84.5 6.5 %copy-start.1 = (f32[12,2048]{1,0:T(8,128)S(1)}, f32[12,2048]{1,0:T(8,128)}, u32[]{:S(2)}) copy-start(f32[12,2048]{1,0:T(8,128)} %state_ref.3) | copy-start | bytes 294916
  84.5 6.5 %copy-start.3 = (s32[10240]{0:T(1024)S(1)}, s32[10240]{0:T(1024)}, u32[]{:S(2)}) copy-start(s32[10240]{0:T(1024)} %param.9) | copy-start | bytes 122884
  84.5 6.5 %copy-start.5 = (s32[2048]{0:T(1024)S(1)}, s32[2048]{0:T(1024)}, u32[]{:S(2)}) copy-start(s32[2048]{0:T(1024)} %param.8) | copy-start | bytes 24580
  84.5 6.5 %copy-start.7 = (s32[2048]{0:T(1024)S(1)}, s32[2048]{0:T(1024)}, u32[]{:S(2)}) copy-start(s32[2048]{0:T(1024)} %param.7) | copy-start | bytes 24580

commit v2 on v1

--- a/solution.py
+++ b/solution.py
@@ -17,6 +17,8 @@
 PER = MAIN + TAIL
 FIELD = 8 * TILES
 CHUNK = 512
+ROWS = 16
+BLOCKS = PER // ROWS
 
 f32, bf16 = jnp.float32, jnp.bfloat16
 
@@ -66,7 +68,14 @@
     return ((lax.axis_index("z") * X + lax.axis_index("x")) * C + lax.axis_index("c")) * (TILES * 128)
 
 
-def pick_kernel(state_ref, mass_ref, ticks_ref, levels_ref, active_ref, msg_ref, table_ref):
+def pick_kernel(*refs):
+    given, msg_ref, table_ref, held, sems = refs[:5], refs[5], refs[6], refs[7:12], refs[12]
+    copies = [pltpu.make_async_copy(a, b, sems.at[n]) for n, (a, b) in enumerate(zip(given, held))]
+    for copy in copies:
+        copy.start()
+    for copy in copies:
+        copy.wait()
+    state_ref, mass_ref, ticks_ref, levels_ref, active_ref = held
     start = first_star()
     block = lax.axis_index("aa") * 10
     zero = jnp.zeros((1, 128), f32)
@@ -117,7 +126,7 @@
     keep_ref[8:16, :] = step
 
 
-def force_kernel(targets_ref, got_ref, keep_ref, out_ref, seen_ref, weight_ref, left0_ref, left1_ref, sums_ref):
+def force_kernel(targets_ref, got_ref, keep_ref, out_ref, seen_ref, weight_ref, sums_ref):
     target = targets_ref[0]
     for z in range(1, targets_ref.shape[0]):
         target = target + targets_ref[z]
@@ -146,46 +155,52 @@
     lax.fori_loop(0, GROUPS, weigh, 0)
     sums_ref[...] = jnp.zeros_like(sums_ref)
 
-    def fill(left_ref, chunk):
-        per_group = TILES * 128 // CHUNK
-        g, part = chunk // per_group, chunk % per_group
-        for j in range(CHUNK // 128):
-            base = pl.multiple_of(part * (CHUNK // 16) + j * 8, 8)
-            star = [jnp.broadcast_to(got_ref[g, pl.ds(base + q, 1), :], (16, 128)) for q in range(6)]
-            for b in range(PER // 16):
-                r = slice(b * 16, (b + 1) * 16)
-                dx, dy, dz, wx, wy, wz = [star[q] - seen_ref[q, r, :] for q in range(6)]
-                total = (dx * dx + EPS2) + dy * dy + dz * dz
-                along = dx * wx + dy * wy + dz * wz
-                inverse = lax.rsqrt(total)
-                square = inverse * inverse
-                cube = square * inverse
-                rate = cube * (square * along)
-                cube_high = cube.astype(bf16)
-                cube_low = (cube - cube_high.astype(f32)).astype(bf16)
-                rate_high = rate.astype(bf16)
-                rate_low = (rate - rate_high.astype(f32)).astype(bf16)
-                for n, part_value in enumerate((cube_high, cube_low, rate_high, rate_low)):
-                    left_ref[n * PER + b * 16 : n * PER + (b + 1) * 16, j * 128 : (j + 1) * 128] = part_value
-
-    def gather(left_ref, chunk):
-        weight = weight_ref[:, pl.ds(pl.multiple_of(chunk * CHUNK, CHUNK), CHUNK)]
-        sums_ref[...] += lax.dot_general(left_ref[...], weight, (((1,), (1,)), ((), ())), preferred_element_type=f32)
-
-    chunks = GROUPS * TILES * 128 // CHUNK
-    fill(left0_ref, 0)
-
-    def body(n, _):
-        fill(left1_ref, 2 * n + 1)
-        gather(left0_ref, 2 * n)
-        fill(left0_ref, jnp.minimum(2 * n + 2, chunks - 1))
-        gather(left1_ref, 2 * n + 1)
+    def chunk(n, _):
+        g, part = n // (TILES * 128 // CHUNK), n % (TILES * 128 // CHUNK)
+        base = pl.multiple_of(part * (CHUNK // 16), 8)
+        across = CHUNK // 128
+        star = [
+            jnp.concatenate(
+                [jnp.broadcast_to(got_ref[g, pl.ds(base + j * 8 + q, 1), :], (ROWS, 128)) for j in range(across)], axis=1
+            )
+            for q in range(6)
+        ]
+        weight = weight_ref[:, pl.ds(pl.multiple_of(n * CHUNK, CHUNK), CHUNK)]
+        values = []
+        for b in range(BLOCKS):
+            r = slice(b * ROWS, (b + 1) * ROWS)
+            seen = [jnp.concatenate([seen_ref[q, r, :]] * across, axis=1) for q in range(6)]
+            dx, dy, dz, wx, wy, wz = [star[q] - seen[q] for q in range(6)]
+            total = (dx * dx + EPS2) + dy * dy + dz * dz
+            along = dx * wx + dy * wy + dz * wz
+            inverse = lax.rsqrt(total)
+            square = inverse * inverse
+            cube = square * inverse
+            rate = cube * (square * along)
+            for value in (cube, rate):
+                high = value.astype(bf16)
+                values += [high, (value - high.astype(f32)).astype(bf16)]
+            if (b + 1) * 4 * ROWS % 256 == 0 or b == BLOCKS - 1:
+                right = jnp.concatenate(values, axis=0)
+                values = []
+                end = (b + 1) * 4 * ROWS
+                sums_ref[:, end - right.shape[0] : end] += lax.dot_general(
+                    weight, right, (((1,), (1,)), ((), ())), preferred_element_type=f32
+                )
         return 0
 
-    lax.fori_loop(0, chunks // 2, body, 0)
-
-    def columns_of(first):
-        total = sums_ref[first : first + PER, :] + sums_ref[first + PER : first + 2 * PER, :]
+    lax.fori_loop(0, GROUPS * TILES * 128 // CHUNK, chunk, 0, unroll=4)
+    sums = jnp.transpose(sums_ref[...])
+
+    def columns_of(part):
+        total = jnp.concatenate(
+            [
+                sums[b * 4 * ROWS + part * ROWS : b * 4 * ROWS + (part + 1) * ROWS]
+                + sums[b * 4 * ROWS + (part + 1) * ROWS : b * 4 * ROWS + (part + 2) * ROWS]
+                for b in range(BLOCKS)
+            ],
+            axis=0,
+        )
         main = jnp.transpose(total[0:MAIN])
         tail = jnp.transpose(total[MAIN:PER])
         return main[0:8] + main[8:16] + main[16:24], tail[0:8] + tail[8:16] + tail[16:24]
@@ -197,7 +212,7 @@
     cube_pos = pack(main[0:3], tail[0:3])
     cube_vel = pack(main[3:6], tail[3:6])
     cube_one = pack(three(main[6:7]), three(tail[6:7]))
-    main, tail = columns_of(2 * PER)
+    main, tail = columns_of(2)
     rate_pos = pack(main[0:3], tail[0:3])
     rate_one = pack(three(main[6:7]), three(tail[6:7]))
     acc = cube_pos - target[0:4] * cube_one
@@ -226,7 +241,7 @@
         out_ref[d, 8:16, :] = both
 
 
-def store_kernel(state_ref, ticks_ref, levels_ref, active_ref, got_ref, new_active_ref, new_state_ref, left_ref, low_ref, sums_ref):
+def store_kernel(state_ref, ticks_ref, levels_ref, active_ref, got_ref, new_active_ref, new_state_ref, sums_ref):
     start = first_star()
     mine = lax.axis_index("aa")
 
@@ -256,24 +271,29 @@
     sums_ref[...] = jnp.zeros_like(sums_ref)
 
     def block(y, _):
-        def put(k, value):
-            local = active_ref[pl.ds(y * 10 + k, 1), :] - start
-            high = jnp.broadcast_to(jnp.right_shift(local, 7), (16, 128))
-            low = jnp.bitwise_and(local, 127)
-            lanes = slice(k * 128, (k + 1) * 128)
-            low_ref[:, lanes] = jnp.where(rows == low, 1.0, 0.0).astype(bf16)
-            first = value.astype(bf16).astype(f32)
-            both = jnp.concatenate([first, value - first], axis=0)
-            for h in range(TILES):
-                left_ref[h * 16 : (h + 1) * 16, lanes] = jnp.where(high == h, both, 0.0).astype(bf16)
-
+        tiles = [jnp.where(row8 == 3, 1.0, got_ref[c, y * X + x, 0:8, :]) for c in range(C) for x in range(X)]
         for c in range(C):
-            for x in range(X):
-                put(c * X + x, jnp.where(row8 == 3, 1.0, got_ref[c, y * X + x, 0:8, :]))
-            put(8 + c, jnp.concatenate([tails(c, y, 3), one, tails(c, y, 7), one], axis=0))
-        sums_ref[...] += lax.dot_general(
-            left_ref[...], low_ref[...], (((1,), (1,)), ((), ())), preferred_element_type=f32
-        )
+            tiles.append(jnp.concatenate([tails(c, y, 3), one, tails(c, y, 7), one], axis=0))
+        total = None
+        for pair in range(5):
+            lefts, lows = [], []
+            for k in (2 * pair, 2 * pair + 1):
+                local = active_ref[pl.ds(y * 10 + k, 1), :] - start
+                high = jnp.broadcast_to(jnp.right_shift(local, 7), (16, 128))
+                lows.append(jnp.where(rows == jnp.bitwise_and(local, 127), 1.0, 0.0).astype(bf16))
+                first = tiles[k].astype(bf16).astype(f32)
+                both = jnp.concatenate([first, tiles[k] - first], axis=0)
+                lefts.append(
+                    jnp.concatenate([jnp.where(high == h, both, 0.0).astype(bf16) for h in range(TILES)], axis=0)
+                )
+            product = lax.dot_general(
+                jnp.concatenate(lefts, axis=1),
+                jnp.concatenate(lows, axis=1),
+                (((1,), (1,)), ((), ())),
+                preferred_element_type=f32,
+            )
+            total = product if total is None else total + product
+        sums_ref[...] += total
         return 0
 
     lax.fori_loop(0, got_ref.shape[1] // X, block, 0)
@@ -300,11 +320,13 @@
     message = pl.pallas_call(
         pick_kernel,
         out_shape=jax.ShapeDtypeStruct((GROUPS, FIELD + 16, 128), f32),
-        in_specs=vmem(5),
+        in_specs=[pl.BlockSpec(memory_space=pltpu.HBM)] * 5,
         out_specs=vmem(1)[0],
-        scratch_shapes=[pltpu.VMEM((768, 128), bf16)],
-        compiler_params=params(),
-    )(state, mass, ticks, levels, active)
+        scratch_shapes=[pltpu.VMEM((768, 128), bf16)]
+        + [pltpu.VMEM(a.shape, a.dtype) for a in (state, mass, ticks, levels, active)]
+        + [pltpu.SemaphoreType.DMA((5,))],
+        compiler_params=params(),
+    )(*[pltpu.with_memory_space_constraint(a, pltpu.HBM) for a in (state, mass, ticks, levels, active)])
     got = lax.all_to_all(message, ("c", "x"), 0, 0, tiled=True)
 
     targets, keep = pl.pallas_call(
@@ -328,9 +350,7 @@
         scratch_shapes=[
             pltpu.VMEM((6, PER, 128), f32),
             pltpu.VMEM((32, GROUPS * TILES * 128), bf16),
-            pltpu.VMEM((4 * PER, CHUNK), bf16),
-            pltpu.VMEM((4 * PER, CHUNK), bf16),
-            pltpu.VMEM((4 * PER, 32), f32),
+            pltpu.VMEM((32, 4 * PER), f32),
         ],
         compiler_params=params(),
     )(targets, got, keep)
@@ -352,8 +372,6 @@
         in_specs=vmem(5),
         out_specs=vmem(2),
         scratch_shapes=[
-            pltpu.VMEM((256, 1280), bf16),
-            pltpu.VMEM((128, 1280), bf16),
             pltpu.VMEM((256, 128), f32),
         ],
         compiler_params=params(),

time: 95.8 us -> 86 us (0.90)
  Pallas kernels: 23.7 us -> 17.8 us
  local copies, waits for them, and re-layouts: 3.78 us -> 0.01 us
    pallas_call x1, Pallas kernels: 18.3 us -> 11.9 us  [per_device(): pl.pallas_call(force_kernel, out_shape=jax.ShapeDtypeStruct((z_count, 24,...]
    unnamed x18 -> x8, local copies, waits for them, and re-layouts: 3.78 us -> 0.01 us
    pallas_call x1, Pallas kernels: 0.87 us -> 1.84 us  [per_device(): pl.pallas_call(pick_kernel, out_shape=jax.ShapeDtypeStruct((GROUPS, FIELD...]
where the time goes in v2:
time: 86 us; the launch traced here: 85.7 us
  blocking collectives  67.3 us (78%)
  Pallas kernels  17.8 us (21%)
    all_to_all x1, blocking collectives, per_device(): got = lax.all_to_all(message, ('c', 'x'), 0, 0, tiled=True)  19.7 us
    all_to_all x1, blocking collectives, per_device(): updates = lax.all_to_all(updates, ('aa', 'x'), 0, 0, tiled=True)  18 us
    all_to_all x1, blocking collectives, per_device(): targets = lax.all_to_all(targets, 'z', 0, 0, tiled=True)  13.2 us
    pallas_call x1, Pallas kernels, per_device(): pl.pallas_call(force_kernel, out_shape=jax.ShapeDtypeStruct((z_count, 24,...  11.9 us
    all_to_all x1, blocking collectives, per_device(): partial = lax.all_to_all(partial, 'z', 0, 0, tiled=True)  9.96 us
    all_gather x1, blocking collectives, per_device(): updates = lax.all_gather(updates, 'c')  6.49 us
    pallas_call x1, Pallas kernels, per_device(): pl.pallas_call(store_kernel, out_shape=[jax.ShapeDtypeStruct((12, 1280),...  3.92 us
    pallas_call x1, Pallas kernels, per_device(): pl.pallas_call(pick_kernel, out_shape=jax.ShapeDtypeStruct((GROUPS, FIELD...  1.84 us

profile of v2, /device:TPU:1, one launch (start us, length us, event | category | flops | bytes accessed | tf_op | source)
XLA Modules:
  0.0 85.7 jit_solution(13016371593111259403)
XLA Ops:
  0.6 1.8 %shard_map.68 = f32[8,144,128]{2,1,0:T(8,128)S(1)} custom-call(f32[12,2048]{1,0:T(8,128)} %state_ref.1, f32[16,128]{1,0:T(8,128)} %bitcast.12, s32[16,128]{1,0:T(8,128)} %bitcast.8, s32[16,128]{1,0:T(8,128)} %bitcast.10, s32[80,128]{1,0:T(8,128)} %bitcast.6), custom_call_target="tpu_custom_call" | custom-call | tf_op jit(solution)/shard_map/pallas_call | solution.py:320
  2.5 19.7 %all_to_all.20.got_ref.first_ref = f32[8,144,128]{2,1,0:T(8,128)S(1)} all-to-all(f32[8,144,128]{2,1,0:T(8,128)S(1)} %shard_map.68), channel_id=1, replica_groups=mesh['z'=8,'x'=4,'c'=2,'aa'=8] {'c','x'}, dimensions={0} | all-to-all | bytes 1179648 | tf_op jit(solution)/shard_map/all_to_all | solution.py:330
  22.1 13.2 %all_to_all.21.targets_ref.refs_0_ = f32[8,8,128]{2,1,0:T(8,128)S(1)} all-to-all(f32[8,8,128]{2,1,0:T(8,128)S(1)} %get-tuple-element.4), channel_id=1, replica_groups=mesh['z'=8,'x'=4,'c'=2,'aa'=8] {'z'}, dimensions={0} | all-to-all | bytes 65536 | tf_op jit(solution)/shard_map/all_to_all | solution.py:343
  35.3 11.9 %shard_map.70 = f32[8,24,128]{2,1,0:T(8,128)S(1)} custom-call(f32[8,8,128]{2,1,0:T(8,128)S(1)} %all_to_all.21.targets_ref.refs_0_, f32[8,144,128]{2,1,0:T(8,128)S(1)} %all_to_all.20.got_ref.first_ref, f32[16,128]{1,0:T(8,128)S(1)} %get-tuple-element.5.keep_ref), custom_call_target="tpu_custom_call" | custom-call | tf_op jit(solution)/shard_map/pallas_call | solution.py:345
  47.2 10.0 %all_to_all.22.refs_1_ = f32[8,24,128]{2,1,0:T(8,128)S(1)} all-to-all(f32[8,24,128]{2,1,0:T(8,128)S(1)} %shard_map.70), channel_id=1, replica_groups=mesh['z'=8,'x'=4,'c'=2,'aa'=8] {'z'}, dimensions={0} | all-to-all | bytes 196608 | tf_op jit(solution)/shard_map/all_to_all | solution.py:357
  57.2 0.1 shard_map.71
  57.3 18.0 %all_to_all.23 = f32[32,16,128]{2,1,0:T(8,128)S(1)} all-to-all(f32[32,16,128]{2,1,0:T(8,128)S(1)} %shard_map.71), channel_id=1, replica_groups=mesh['z'=8,'x'=4,'c'=2,'aa'=8] {'aa','x'}, dimensions={0} | all-to-all | bytes 524288 | tf_op jit(solution)/shard_map/all_to_all | solution.py:366
  75.3 0.0 copy-start
  75.3 0.0 copy-start.1
  75.3 0.0 copy-start.2
  75.3 0.0 copy-start.3
  75.3 6.5 %all-gather = f32[64,16,128]{2,1,0:T(8,128)S(1)} all-gather(f32[32,16,128]{2,1,0:T(8,128)S(1)} %all_to_all.23), channel_id=2, replica_groups=mesh['z'=8,'x'=4,'c'=2,'aa'=8] {'c'}, dimensions={0}, use_global_device_ids=true | all-gather | bytes 786432 | tf_op jit(solution)/shard_map/all_gather | solution.py:367
  81.8 0.0 copy-done
  81.8 0.0 copy-done.1
  81.8 0.0 copy-done.2
  81.8 0.0 copy-done.3
  81.8 3.9 %shard_map.72 = (f32[12,1280]{1,0:T(8,128)}, f32[12,2048]{1,0:T(8,128)}) custom-call(f32[12,2048]{1,0:T(8,128)S(1)} %copy-done, s32[16,128]{1,0:T(8,128)S(1)} %bitcast.9, s32[16,128]{1,0:T(8,128)S(1)} %bitcast.11, s32[80,128]{1,0:T(8,128)S(1)} %bitcast.7, f32[2,32,16,128]{3,2,1,0:T(8,128)S(1)} %bitcast.5), custom_call_target="tpu_custom_call" | custom-call | tf_op jit(solution)/shard_map/pallas_call | solution.py:369
  (1 shorter events, 0.0 us)
Async XLA Ops:
  75.3 6.5 %copy-start = (f32[12,2048]{1,0:T(8,128)S(1)}, f32[12,2048]{1,0:T(8,128)}, u32[]{:S(2)}) copy-start(f32[12,2048]{1,0:T(8,128)} %state_ref.1) | copy-start | bytes 294916
  75.3 6.5 %copy-start.1 = (s32[10240]{0:T(1024)S(1)}, s32[10240]{0:T(1024)}, u32[]{:S(2)}) copy-start(s32[10240]{0:T(1024)} %param.9) | copy-start | bytes 122884
  75.3 6.5 %copy-start.2 = (s32[2048]{0:T(1024)S(1)}, s32[2048]{0:T(1024)}, u32[]{:S(2)}) copy-start(s32[2048]{0:T(1024)} %param.8) | copy-start | bytes 24580
  75.3 6.5 %copy-start.3 = (s32[2048]{0:T(1024)S(1)}, s32[2048]{0:T(1024)}, u32[]{:S(2)}) copy-start(s32[2048]{0:T(1024)} %param.7) | copy-start | bytes 24580

commit v3 on v2

--- a/solution.py
+++ b/solution.py
@@ -88,8 +88,8 @@
         both = jnp.concatenate([field, s[6:12], step, zero], axis=0)
         for n, part in enumerate(split3(both)):
             table_ref[n * 256 + i * 16 : n * 256 + (i + 1) * 16, :] = part
-        for g in range(GROUPS):
-            msg_ref[g, i * 8 : (i + 1) * 8, :] = field
+        for x in range(X):
+            msg_ref[x, i * 8 : (i + 1) * 8, :] = field
     rows = lax.broadcasted_iota(jnp.int32, (128, 128), 0)
     picks = []
     for k in range(10):
@@ -107,23 +107,25 @@
     for g in range(GROUPS):
         main = picks[g]
         tail = picks[8 + g // 4][:, (g % 4) * TAIL : (g % 4 + 1) * TAIL]
-        msg_ref[g, FIELD : FIELD + 4, :] = pack(main[0:3], tail[0:3])
-        msg_ref[g, FIELD + 4 : FIELD + 8, :] = pack(main[3:6], tail[3:6])
-        msg_ref[g, FIELD + 8 : FIELD + 12, :] = pack(main[8:11], tail[8:11], tail[14:15])
-        msg_ref[g, FIELD + 12 : FIELD + 16, :] = pack(main[11:14], tail[11:14])
-        msg_ref[g, 7:8, :] = main[14:15]
-
-
-def sum_kernel(got_ref, first_ref, out_ref, keep_ref):
-    total = got_ref[0]
-    step = first_ref[0]
+        step = [main[14:15, n * TAIL : (n + 1) * TAIL] for n in range(4)]
+        x, row = g % X, FIELD + 16 * (g // X)
+        for n, q in enumerate((0, 3, 8, 11)):
+            msg_ref[x, row + 4 * n : row + 4 * n + 4, :] = pack(main[q : q + 3], tail[q : q + 3], step[n])
+        msg_ref[x, 8 * (g // X) + 7 : 8 * (g // X) + 8, :] = jnp.concatenate([tail[14:15], jnp.zeros((1, 96), f32)], axis=1)
+
+
+def sum_kernel(got_ref, out_ref, keep_ref):
+    c = lax.axis_index("c")
+    picks = pl.ds(pl.multiple_of(FIELD + 16 * c, 16), 16)
+    total = got_ref[0, picks, :]
+    step = got_ref[0, pl.ds(8 * c + 7, 1), :]
     for g in range(1, GROUPS):
-        total = total + got_ref[g]
-        step = step + first_ref[g]
+        total = total + got_ref[g, picks, :]
+        step = step + got_ref[g, pl.ds(8 * c + 7, 1), :]
     for z in range(out_ref.shape[0]):
         out_ref[z] = total[0:8]
     keep_ref[0:8, :] = total[8:16]
-    keep_ref[8:16, :] = step
+    keep_ref[8:16, :] = jnp.broadcast_to(step, (8, 128))
 
 
 def force_kernel(targets_ref, got_ref, keep_ref, out_ref, seen_ref, weight_ref, sums_ref):
@@ -217,10 +219,11 @@
     rate_one = pack(three(main[6:7]), three(tail[6:7]))
     acc = cube_pos - target[0:4] * cube_one
     jerk = (cube_vel - target[4:8] * cube_one) - 3.0 * (rate_pos - target[0:4] * rate_one)
-    forces = jnp.concatenate([acc, jerk], axis=0)
+    last = jnp.concatenate([acc[3:4, 0:96], keep_ref[8:9, 0:TAIL]], axis=1)
+    forces = jnp.concatenate([acc[0:3], last, jerk], axis=0)
     for z in range(out_ref.shape[0]):
         out_ref[z, 0:8, :] = forces
-        out_ref[z, 8:24, :] = keep_ref[...]
+        out_ref[z, 8:16, :] = keep_ref[0:8, :]
 
 
 def correct_kernel(scale, targets_ref, got_ref, out_ref):
@@ -231,8 +234,8 @@
         total = total + got_ref[z]
     forces = total[0:8] * scale
     old = total[8:16]
-    main = total[23:24]
-    tail = old[3:4, 96:128]
+    main = jnp.concatenate([a[r : r + 1, 96:128] for a in (target, old) for r in (3, 7)], axis=1)
+    tail = total[3:4, 96:128]
     step = pack(jnp.concatenate([main, main, main], axis=0), jnp.concatenate([tail, tail, tail], axis=0))
     pos, vel = correct(target[0:4], target[4:8], old[0:4], old[4:8], step, forces[0:4], forces[4:8])
     both = jnp.concatenate([pos, vel], axis=0)
@@ -246,7 +249,7 @@
     mine = lax.axis_index("aa")
 
     def tails(c, y, row):
-        parts = [got_ref[c, y * X + x, row : row + 1, :] for x in range(X)]
+        parts = [got_ref[c * X + x, y, row : row + 1, :] for x in range(X)]
         return jnp.concatenate(
             [jnp.concatenate([p[:, q * TAIL : (q + 1) * TAIL] for p in parts], axis=1) for q in range(3)], axis=0
         )
@@ -254,7 +257,7 @@
     for c in range(C):
         for x in range(X):
             lanes = slice((c * X + x) * 128, (c * X + x + 1) * 128)
-            tile = got_ref[c, mine * X + x]
+            tile = got_ref[c * X + x, mine]
             new_active_ref[0:3, lanes] = tile[8:11]
             new_active_ref[3:6, lanes] = tile[12:15]
             new_active_ref[6:9, lanes] = tile[0:3]
@@ -271,32 +274,27 @@
     sums_ref[...] = jnp.zeros_like(sums_ref)
 
     def block(y, _):
-        tiles = [jnp.where(row8 == 3, 1.0, got_ref[c, y * X + x, 0:8, :]) for c in range(C) for x in range(X)]
+        tiles = [jnp.where(row8 == 3, 1.0, got_ref[c * X + x, y, 0:8, :]) for c in range(C) for x in range(X)]
         for c in range(C):
             tiles.append(jnp.concatenate([tails(c, y, 3), one, tails(c, y, 7), one], axis=0))
-        total = None
-        for pair in range(5):
-            lefts, lows = [], []
-            for k in (2 * pair, 2 * pair + 1):
-                local = active_ref[pl.ds(y * 10 + k, 1), :] - start
-                high = jnp.broadcast_to(jnp.right_shift(local, 7), (16, 128))
-                lows.append(jnp.where(rows == jnp.bitwise_and(local, 127), 1.0, 0.0).astype(bf16))
-                first = tiles[k].astype(bf16).astype(f32)
-                both = jnp.concatenate([first, tiles[k] - first], axis=0)
-                lefts.append(
-                    jnp.concatenate([jnp.where(high == h, both, 0.0).astype(bf16) for h in range(TILES)], axis=0)
-                )
-            product = lax.dot_general(
-                jnp.concatenate(lefts, axis=1),
-                jnp.concatenate(lows, axis=1),
-                (((1,), (1,)), ((), ())),
-                preferred_element_type=f32,
-            )
-            total = product if total is None else total + product
+        lefts, lows = [], []
+        for k, tile in enumerate(tiles):
+            local = active_ref[pl.ds(y * 10 + k, 1), :] - start
+            high = jnp.broadcast_to(jnp.right_shift(local, 7), (16, 128))
+            lows.append(jnp.where(rows == jnp.bitwise_and(local, 127), 1.0, 0.0).astype(bf16))
+            first = tile.astype(bf16).astype(f32)
+            both = jnp.concatenate([first, tile - first], axis=0)
+            lefts.append(jnp.concatenate([jnp.where(high == h, both, 0.0).astype(bf16) for h in range(TILES)], axis=0))
+        total = lax.dot_general(
+            jnp.concatenate(lefts, axis=1),
+            jnp.concatenate(lows, axis=1),
+            (((1,), (1,)), ((), ())),
+            preferred_element_type=f32,
+        )
         sums_ref[...] += total
         return 0
 
-    lax.fori_loop(0, got_ref.shape[1] // X, block, 0)
+    lax.fori_loop(0, got_ref.shape[1], block, 0, unroll=4)
 
     for i in range(TILES):
         lanes = slice(i * 128, (i + 1) * 128)
@@ -319,7 +317,7 @@
 
     message = pl.pallas_call(
         pick_kernel,
-        out_shape=jax.ShapeDtypeStruct((GROUPS, FIELD + 16, 128), f32),
+        out_shape=jax.ShapeDtypeStruct((X, FIELD + 16 * C, 128), f32),
         in_specs=[pl.BlockSpec(memory_space=pltpu.HBM)] * 5,
         out_specs=vmem(1)[0],
         scratch_shapes=[pltpu.VMEM((768, 128), bf16)]
@@ -327,24 +325,21 @@
         + [pltpu.SemaphoreType.DMA((5,))],
         compiler_params=params(),
     )(*[pltpu.with_memory_space_constraint(a, pltpu.HBM) for a in (state, mass, ticks, levels, active)])
-    got = lax.all_to_all(message, ("c", "x"), 0, 0, tiled=True)
+    got = lax.all_to_all(message, "x", 0, 0, tiled=True)
+    got = lax.all_gather(got, "c", tiled=True)
 
     targets, keep = pl.pallas_call(
         sum_kernel,
-        grid=(1,),
         out_shape=[jax.ShapeDtypeStruct((z_count, 8, 128), f32), jax.ShapeDtypeStruct((16, 128), f32)],
-        in_specs=[
-            pl.BlockSpec((GROUPS, 16, 128), lambda i: (0, FIELD // 16, 0)),
-            pl.BlockSpec((GROUPS, 8, 128), lambda i: (0, 0, 0)),
-        ],
-        out_specs=[pl.BlockSpec((z_count, 8, 128), lambda i: (0, 0, 0)), pl.BlockSpec((16, 128), lambda i: (0, 0))],
-        compiler_params=params(),
-    )(got, got)
+        in_specs=vmem(1),
+        out_specs=vmem(2),
+        compiler_params=params(),
+    )(got)
     targets = lax.all_to_all(targets, "z", 0, 0, tiled=True)
 
     partial = pl.pallas_call(
         force_kernel,
-        out_shape=jax.ShapeDtypeStruct((z_count, 24, 128), f32),
+        out_shape=jax.ShapeDtypeStruct((z_count, 16, 128), f32),
         in_specs=vmem(3),
         out_specs=vmem(1)[0],
         scratch_shapes=[
@@ -363,8 +358,8 @@
         out_specs=vmem(1)[0],
         compiler_params=params(),
     )(targets, partial)
-    updates = lax.all_to_all(updates, ("aa", "x"), 0, 0, tiled=True)
-    updates = lax.all_gather(updates, "c")
+    updates = lax.all_to_all(updates, ("x", "aa"), 0, 0, tiled=True)
+    updates = lax.all_gather(updates, "c", tiled=True).reshape(GROUPS, y_count, 16, 128)
 
     new_active, new_state = pl.pallas_call(
         store_kernel,

time: 86 us -> 82.6 us (0.960)
  blocking collectives: 67.3 us -> 64.9 us
  Pallas kernels: 17.8 us -> 16.8 us
    all_to_all x2, blocking collectives: 37.7 us -> 27.8 us  [the longest x1 17.3 us: per_device(): updates = lax.all_to_all(updates, ('x', 'aa'), 0, 0, tiled=True)]
    all_gather x1 -> x2, blocking collectives: 6.49 us -> 13.9 us  [the longest x1 7.65 us: per_device(): got = lax.all_gather(got, 'c', tiled=True)]
    pallas_call x1, Pallas kernels: 3.92 us -> 2.79 us  [per_device(): pl.pallas_call(store_kernel, out_shape=[jax.ShapeDtypeStruct((12, 1280),...]
where the time goes in v3:
time: 82.6 us; the launch traced here: 82.4 us
  blocking collectives  64.9 us (79%)
  Pallas kernels  16.8 us (20%)
    all_to_all x1, blocking collectives, per_device(): updates = lax.all_to_all(updates, ('x', 'aa'), 0, 0, tiled=True)  17.3 us
    all_to_all x1, blocking collectives, per_device(): targets = lax.all_to_all(targets, 'z', 0, 0, tiled=True)  13.5 us
    pallas_call x1, Pallas kernels, per_device(): pl.pallas_call(force_kernel, out_shape=jax.ShapeDtypeStruct((z_count, 16,...  12 us
    all_to_all x1, blocking collectives, per_device(): got = lax.all_to_all(message, 'x', 0, 0, tiled=True)  10.5 us
    all_to_all x1, blocking collectives, per_device(): partial = lax.all_to_all(partial, 'z', 0, 0, tiled=True)  9.7 us
    all_gather x1, blocking collectives, per_device(): got = lax.all_gather(got, 'c', tiled=True)  7.65 us
    all_gather x1, blocking collectives, per_device(): lax.all_gather(updates, 'c', tiled=True).reshape(GROUPS, y_count, 16, 128)  6.28 us
    pallas_call x1, Pallas kernels, per_device(): pl.pallas_call(store_kernel, out_shape=[jax.ShapeDtypeStruct((12, 1280),...  2.79 us

profile of v3, /device:TPU:1, one launch (start us, length us, event | category | flops | bytes accessed | tf_op | source)
XLA Modules:
  0.0 82.4 jit_solution(17628896682964816767)
XLA Ops:
  0.6 1.8 %shard_map.68 = f32[4,160,128]{2,1,0:T(8,128)S(1)} custom-call(f32[12,2048]{1,0:T(8,128)} %state_ref.1, f32[16,128]{1,0:T(8,128)} %bitcast.12, s32[16,128]{1,0:T(8,128)} %bitcast.8, s32[16,128]{1,0:T(8,128)} %bitcast.10, s32[80,128]{1,0:T(8,128)} %bitcast.6), custom_call_target="tpu_custom_call" | custom-call | tf_op jit(solution)/shard_map/pallas_call | solution.py:318
  2.5 10.5 %all_to_all.20 = f32[4,160,128]{2,1,0:T(8,128)S(1)} all-to-all(f32[4,160,128]{2,1,0:T(8,128)S(1)} %shard_map.68), channel_id=1, replica_groups=mesh['z'=8,'x'=4,'c'=2,'aa'=8] {'x'}, dimensions={0} | all-to-all | bytes 655360 | tf_op jit(solution)/shard_map/all_to_all | solution.py:328
  13.0 7.6 %all_gather.6.got_ref = f32[8,160,128]{2,1,0:T(8,128)S(1)} all-gather(f32[4,160,128]{2,1,0:T(8,128)S(1)} %all_to_all.20), channel_id=1, replica_groups=mesh['z'=8,'x'=4,'c'=2,'aa'=8] {'c'}, dimensions={0}, use_global_device_ids=true | all-gather | bytes 983040 | tf_op jit(solution)/shard_map/all_gather | solution.py:329
  20.7 13.5 %all_to_all.21.targets_ref.refs_0_ = f32[8,8,128]{2,1,0:T(8,128)S(1)} all-to-all(f32[8,8,128]{2,1,0:T(8,128)S(1)} %get-tuple-element.4), channel_id=1, replica_groups=mesh['z'=8,'x'=4,'c'=2,'aa'=8] {'z'}, dimensions={0} | all-to-all | bytes 65536 | tf_op jit(solution)/shard_map/all_to_all | solution.py:338
  34.1 12.0 %shard_map.70 = f32[8,16,128]{2,1,0:T(8,128)S(1)} custom-call(f32[8,8,128]{2,1,0:T(8,128)S(1)} %all_to_all.21.targets_ref.refs_0_, f32[8,160,128]{2,1,0:T(8,128)S(1)} %all_gather.6.got_ref, f32[16,128]{1,0:T(8,128)S(1)} %get-tuple-element.5.keep_ref), custom_call_target="tpu_custom_call" | custom-call | tf_op jit(solution)/shard_map/pallas_call | solution.py:340
  46.2 9.7 %all_to_all.22.refs_1_ = f32[8,16,128]{2,1,0:T(8,128)S(1)} all-to-all(f32[8,16,128]{2,1,0:T(8,128)S(1)} %shard_map.70), channel_id=1, replica_groups=mesh['z'=8,'x'=4,'c'=2,'aa'=8] {'z'}, dimensions={0} | all-to-all | bytes 131072 | tf_op jit(solution)/shard_map/all_to_all | solution.py:352
  55.9 0.1 shard_map.71
  56.0 17.3 %all_to_all.23 = f32[32,16,128]{2,1,0:T(8,128)S(1)} all-to-all(f32[32,16,128]{2,1,0:T(8,128)S(1)} %shard_map.71), channel_id=1, replica_groups=mesh['z'=8,'x'=4,'c'=2,'aa'=8] {'x','aa'}, dimensions={0} | all-to-all | bytes 524288 | tf_op jit(solution)/shard_map/all_to_all | solution.py:361
  73.3 0.0 copy-start
  73.3 0.0 copy-start.1
  73.3 0.0 copy-start.2
  73.3 0.0 copy-start.3
  73.3 6.3 %all_gather.7 = f32[64,16,128]{2,1,0:T(8,128)S(1)} all-gather(f32[32,16,128]{2,1,0:T(8,128)S(1)} %all_to_all.23), channel_id=1, replica_groups=mesh['z'=8,'x'=4,'c'=2,'aa'=8] {'c'}, dimensions={0}, use_global_device_ids=true | all-gather | bytes 786432 | tf_op jit(solution)/shard_map/all_gather | solution.py:362
  79.6 0.0 copy-done
  79.6 0.0 copy-done.1
  79.6 0.0 copy-done.2
  79.6 0.0 copy-done.3
  79.6 2.8 %shard_map.72 = (f32[12,1280]{1,0:T(8,128)}, f32[12,2048]{1,0:T(8,128)}) custom-call(f32[12,2048]{1,0:T(8,128)S(1)} %copy-done, s32[16,128]{1,0:T(8,128)S(1)} %bitcast.9, s32[16,128]{1,0:T(8,128)S(1)} %bitcast.11, s32[80,128]{1,0:T(8,128)S(1)} %bitcast.7, f32[8,8,16,128]{3,2,1,0:T(8,128)S(1)} %bitcast.5), custom_call_target="tpu_custom_call" | custom-call | tf_op jit(solution)/shard_map/pallas_call | solution.py:364
  (1 shorter events, 0.0 us)
Async XLA Ops:
  73.3 6.3 %copy-start = (f32[12,2048]{1,0:T(8,128)S(1)}, f32[12,2048]{1,0:T(8,128)}, u32[]{:S(2)}) copy-start(f32[12,2048]{1,0:T(8,128)} %state_ref.1) | copy-start | bytes 294916
  73.3 6.3 %copy-start.1 = (s32[10240]{0:T(1024)S(1)}, s32[10240]{0:T(1024)}, u32[]{:S(2)}) copy-start(s32[10240]{0:T(1024)} %param.9) | copy-start | bytes 122884
  73.3 6.3 %copy-start.2 = (s32[2048]{0:T(1024)S(1)}, s32[2048]{0:T(1024)}, u32[]{:S(2)}) copy-start(s32[2048]{0:T(1024)} %param.8) | copy-start | bytes 24580
  73.3 6.3 %copy-start.3 = (s32[2048]{0:T(1024)S(1)}, s32[2048]{0:T(1024)}, u32[]{:S(2)}) copy-start(s32[2048]{0:T(1024)} %param.7) | copy-start | bytes 24580

commit v4 on v3

--- a/solution.py
+++ b/solution.py
@@ -128,33 +128,59 @@
     keep_ref[8:16, :] = jnp.broadcast_to(step, (8, 128))
 
 
-def force_kernel(targets_ref, got_ref, keep_ref, out_ref, seen_ref, weight_ref, sums_ref):
+def star_kernel(got_ref, weight_ref, cross_ref, center_ref):
+    row = lax.broadcasted_iota(jnp.int32, (8, 128), 0)
+    center = jnp.broadcast_to(jnp.mean(got_ref[0, 0:8, :], axis=1, keepdims=True), (8, 128))
+    center = jnp.where(row < 6, center, 0.0)
+    center_ref[...] = center
+
+    def group(g, _):
+        for i in range(TILES):
+            lanes = pl.ds(pl.multiple_of((g * TILES + i) * 128, 128), 128)
+            tile = got_ref[g, i * 8 : (i + 1) * 8, :]
+            value = jnp.where(row < 6, tile * tile[6:7], jnp.where(row == 6, tile, 0.0))
+            first = value.astype(bf16).astype(f32)
+            rest = value - first
+            second = rest.astype(bf16).astype(f32)
+            weight_ref[:, lanes] = jnp.concatenate([first, second, rest - second, rest - rest], axis=0).astype(bf16)
+            tile = tile - center
+            dot = jnp.sum(tile[0:3] * tile[3:6], axis=0, keepdims=True)
+            value = jnp.where(row < 6, tile, jnp.where(row == 6, 1.0, dot))
+            first = value.astype(bf16).astype(f32)
+            rest = value - first
+            second = rest.astype(bf16).astype(f32)
+            third = rest - second
+            cross_ref[:, lanes] = jnp.concatenate(
+                [first, second, first, second, third, first, third, second], axis=0
+            ).astype(bf16)
+        return 0
+
+    lax.fori_loop(0, GROUPS, group, 0)
+
+
+def target_rows(pos, vel, center):
+    pos, vel = pos - center[0:3, 0:1], vel - center[3:6, 0:1]
+    value = jnp.concatenate([-vel, -pos, jnp.sum(pos * vel, axis=0, keepdims=True), jnp.ones_like(pos[0:1])], axis=0)
+    first = value.astype(bf16).astype(f32)
+    rest = value - first
+    second = rest.astype(bf16).astype(f32)
+    third = rest - second
+    return jnp.transpose(jnp.concatenate([first, first, second, second, first, third, second, third], axis=0)).astype(bf16)
+
+
+def force_kernel(targets_ref, got_ref, keep_ref, weight_ref, cross_ref, center_ref, out_ref, seen_ref, left_ref, sums_ref):
     target = targets_ref[0]
     for z in range(1, targets_ref.shape[0]):
         target = target + targets_ref[z]
     columns = jnp.transpose(target)
-    for half in range(2):
-        for q in range(3):
-            seen_ref[half * 3 + q, 0:MAIN, :] = jnp.broadcast_to(columns[:, half * 4 + q : half * 4 + q + 1], (MAIN, 128))
-            seen_ref[half * 3 + q, MAIN:PER, :] = jnp.broadcast_to(
-                columns[q * TAIL : (q + 1) * TAIL, half * 4 + 3 : half * 4 + 4], (TAIL, 128)
-            )
-
-    row = lax.broadcasted_iota(jnp.int32, (8, 128), 0)
-
-    def weigh(g, _):
-        for i in range(TILES):
-            tile = got_ref[g, i * 8 : (i + 1) * 8, :]
-            mass = tile[6:7]
-            value = jnp.where(row < 6, tile * mass, jnp.where(row == 6, tile, 0.0))
-            first = value.astype(bf16).astype(f32)
-            rest = value - first
-            second = rest.astype(bf16).astype(f32)
-            rows = jnp.concatenate([first, second, rest - second, jnp.zeros_like(value)], axis=0).astype(bf16)
-            weight_ref[:, pl.ds(pl.multiple_of((g * TILES + i) * 128, 128), 128)] = rows
-        return 0
-
-    lax.fori_loop(0, GROUPS, weigh, 0)
+    for q in range(3):
+        seen_ref[q, 0:MAIN, :] = jnp.broadcast_to(columns[:, q : q + 1], (MAIN, 128))
+        seen_ref[q, MAIN:PER, :] = jnp.broadcast_to(columns[q * TAIL : (q + 1) * TAIL, 3:4], (TAIL, 128))
+    tails = [
+        jnp.concatenate([target[r : r + 1, q * TAIL : (q + 1) * TAIL] for q in range(3)], axis=0) for r in (3, 7)
+    ]
+    left_ref[0:MAIN, :] = target_rows(target[0:3], target[4:7], center_ref[...])
+    left_ref[MAIN:PER, :] = target_rows(tails[0], tails[1], center_ref[...])
     sums_ref[...] = jnp.zeros_like(sums_ref)
 
     def chunk(n, _):
@@ -165,16 +191,17 @@
             jnp.concatenate(
                 [jnp.broadcast_to(got_ref[g, pl.ds(base + j * 8 + q, 1), :], (ROWS, 128)) for j in range(across)], axis=1
             )
-            for q in range(6)
+            for q in range(3)
         ]
-        weight = weight_ref[:, pl.ds(pl.multiple_of(n * CHUNK, CHUNK), CHUNK)]
+        lanes = pl.ds(pl.multiple_of(n * CHUNK, CHUNK), CHUNK)
+        weight = weight_ref[:, lanes]
+        alongs = jnp.dot(left_ref[...], cross_ref[:, lanes], preferred_element_type=f32)
         values = []
         for b in range(BLOCKS):
             r = slice(b * ROWS, (b + 1) * ROWS)
-            seen = [jnp.concatenate([seen_ref[q, r, :]] * across, axis=1) for q in range(6)]
-            dx, dy, dz, wx, wy, wz = [star[q] - seen[q] for q in range(6)]
+            dx, dy, dz = [star[q] - jnp.concatenate([seen_ref[q, r, :]] * across, axis=1) for q in range(3)]
             total = (dx * dx + EPS2) + dy * dy + dz * dz
-            along = dx * wx + dy * wy + dz * wz
+            along = alongs[r]
             inverse = lax.rsqrt(total)
             square = inverse * inverse
             cube = square * inverse
@@ -337,18 +364,32 @@
     )(got)
     targets = lax.all_to_all(targets, "z", 0, 0, tiled=True)
 
+    n_field = GROUPS * TILES * 128
+    stars = pl.pallas_call(
+        star_kernel,
+        out_shape=[
+            jax.ShapeDtypeStruct((32, n_field), bf16),
+            jax.ShapeDtypeStruct((64, n_field), bf16),
+            jax.ShapeDtypeStruct((8, 128), f32),
+        ],
+        in_specs=vmem(1),
+        out_specs=vmem(3),
+        compiler_params=params(),
+        cost_estimate=pl.CostEstimate(flops=n_field * 400, bytes_accessed=n_field * 224, transcendentals=0),
+    )(got)
+
     partial = pl.pallas_call(
         force_kernel,
         out_shape=jax.ShapeDtypeStruct((z_count, 16, 128), f32),
-        in_specs=vmem(3),
+        in_specs=vmem(6),
         out_specs=vmem(1)[0],
         scratch_shapes=[
-            pltpu.VMEM((6, PER, 128), f32),
-            pltpu.VMEM((32, GROUPS * TILES * 128), bf16),
+            pltpu.VMEM((3, PER, 128), f32),
+            pltpu.VMEM((PER, 64), bf16),
             pltpu.VMEM((32, 4 * PER), f32),
         ],
         compiler_params=params(),
-    )(targets, got, keep)
+    )(targets, got, keep, *stars)
     partial = lax.all_to_all(partial, "z", 0, 0, tiled=True)
 
     updates = pl.pallas_call(

time: 82.6 us -> 83.7 us (1.013)
  blocking collectives: 64.9 us -> 51.3 us
  starting transfers between devices: 0 us -> 6.73 us
  waiting for transfers between devices: 0 us -> 5.12 us
  local copies, waits for them, and re-layouts: 0.01 us -> 2.19 us
    all_to_all x1 -> x0, blocking collectives: 13.5 us -> none  [per_device(): targets = lax.all_to_all(targets, 'z', 0, 0, tiled=True)]
    all_to_all x0 -> x1, starting transfers between devices: none -> 6.73 us  [per_device(): targets = lax.all_to_all(targets, 'z', 0, 0, tiled=True)]
    all_to_all x0 -> x1, waiting for transfers between devices: none -> 5.12 us  [per_device(): targets = lax.all_to_all(targets, 'z', 0, 0, tiled=True)]
    unnamed x8 -> x12, local copies, waits for them, and re-layouts: 0.01 us -> 2.19 us
    pallas_call x0 -> x1, Pallas kernels: none -> 0.85 us  [per_device(): pl.pallas_call(star_kernel, out_shape=[jax.ShapeDtypeStruct((32, n_field)...]
    pallas_call x1, Pallas kernels: 12 us -> 11.2 us  [per_device(): pl.pallas_call(force_kernel, out_shape=jax.ShapeDtypeStruct((z_count, 16,...]
  transfers between devices with their start and end apart: 0 -> 1, of which waited for: 0 -> 1; matrix products, arithmetic and copies ran while one was open for 0% -> 0% of each run, Pallas kernels for 0% -> 1%
where the time goes in v4:
time: 83.7 us; the launch traced here: 83.4 us
  blocking collectives  51.3 us (61%)
  Pallas kernels  17.4 us (21%)
  starting transfers between devices  6.73 us (8%)
  waiting for transfers between devices  5.12 us (6%)
  local copies, waits for them, and re-layouts  2.19 us (3%)
    all_to_all x1, blocking collectives, per_device(): updates = lax.all_to_all(updates, ('x', 'aa'), 0, 0, tiled=True)  17.3 us
    pallas_call x1, Pallas kernels, per_device(): pl.pallas_call(force_kernel, out_shape=jax.ShapeDtypeStruct((z_count, 16,...  11.2 us
    all_to_all x1, blocking collectives, per_device(): got = lax.all_to_all(message, 'x', 0, 0, tiled=True)  10.5 us
    all_to_all x1, blocking collectives, per_device(): partial = lax.all_to_all(partial, 'z', 0, 0, tiled=True)  9.7 us
    all_gather x1, blocking collectives, per_device(): got = lax.all_gather(got, 'c', tiled=True)  7.65 us
    all_to_all x1, starting transfers between devices, per_device(): targets = lax.all_to_all(targets, 'z', 0, 0, tiled=True)  6.73 us
    all_gather x1, blocking collectives, per_device(): lax.all_gather(updates, 'c', tiled=True).reshape(GROUPS, y_count, 16, 128)  6.13 us
    all_to_all x1, waiting for transfers between devices, per_device(): targets = lax.all_to_all(targets, 'z', 0, 0, tiled=True)  5.12 us
  transfers between devices with their start and end apart: 1, of which 1 were waited for; matrix products, arithmetic and copies ran while one was open for 0% of the time, Pallas kernels for 1%

profile of v4, /device:TPU:1, one launch (start us, length us, event | category | flops | bytes accessed | tf_op | source)
XLA Modules:
  0.0 83.4 jit_solution(862610725027022760)
XLA Ops:
  0.6 1.8 %shard_map.68 = f32[4,160,128]{2,1,0:T(8,128)S(1)} custom-call(f32[12,2048]{1,0:T(8,128)} %state_ref.1, f32[16,128]{1,0:T(8,128)} %bitcast.12, s32[16,128]{1,0:T(8,128)} %bitcast.8, s32[16,128]{1,0:T(8,128)} %bitcast.10, s32[80,128]{1,0:T(8,128)} %bitcast.6), custom_call_target="tpu_custom_call" | custom-call | tf_op jit(solution)/shard_map/pallas_call | solution.py:345
  2.5 10.5 %all_to_all.20 = f32[4,160,128]{2,1,0:T(8,128)S(1)} all-to-all(f32[4,160,128]{2,1,0:T(8,128)S(1)} %shard_map.68), channel_id=1, replica_groups=mesh['z'=8,'x'=4,'c'=2,'aa'=8] {'x'}, dimensions={0} | all-to-all | bytes 655360 | tf_op jit(solution)/shard_map/all_to_all | solution.py:355
  13.0 7.6 %all_gather.6.got_ref = f32[8,160,128]{2,1,0:T(8,128)S(1)} all-gather(f32[4,160,128]{2,1,0:T(8,128)S(1)} %all_to_all.20), channel_id=1, replica_groups=mesh['z'=8,'x'=4,'c'=2,'aa'=8] {'c'}, dimensions={0}, use_global_device_ids=true | all-gather | bytes 983040 | tf_op jit(solution)/shard_map/all_gather | solution.py:356
  20.6 0.6 shard_map.69
  21.3 6.7 %all-to-all-start.1 = ((f32[8,8,128]{2,1,0:T(8,128)}), f32[8,8,128]{2,1,0:T(8,128)S(1)}, u32[]{:S(2)}, u32[]{:S(2)}) async-start(f32[8,8,128]{2,1,0:T(8,128)} %get-tuple-element.7), calls=%async_computation.1 | async-start | bytes 65536 | tf_op jit(solution)/shard_map/all_to_all | solution.py:365
  28.0 0.9 %shard_map.70 = (bf16[32,16384]{1,0:T(8,128)(2,1)S(1)}, bf16[64,16384]{1,0:T(8,128)(2,1)S(1)}, f32[8,128]{1,0:T(8,128)S(1)}) custom-call(f32[8,160,128]{2,1,0:T(8,128)S(1)} %all_gather.6.got_ref), custom_call_target="tpu_custom_call" | custom-call | flops 6553600 | bytes 3670016 | tf_op jit(solution)/shard_map/pallas_call | solution.py:368
  28.9 0.0 copy-start
  28.9 1.0 %copy-done = bf16[32,16384]{1,0:T(8,128)(2,1)} copy-done((bf16[32,16384]{1,0:T(8,128)(2,1)}, bf16[32,16384]{1,0:T(8,128)(2,1)S(1)}, u32[]{:S(2)}) %copy-start) | copy-done | bytes 1048600
  29.8 5.1 %all-to-all-done.1.targets_ref.refs_0_ = f32[8,8,128]{2,1,0:T(8,128)S(1)} async-done(((f32[8,8,128]{2,1,0:T(8,128)}), f32[8,8,128]{2,1,0:T(8,128)S(1)}, u32[]{:S(2)}, u32[]{:S(2)}) %all-to-all-start.1) | async-done | bytes 32800 | tf_op jit(solution)/shard_map/all_to_all | solution.py:365
  35.0 0.0 copy-start.1
  35.0 1.2 %copy-done.1 = bf16[32,16384]{1,0:T(8,128)(2,1)S(1)} copy-done((bf16[32,16384]{1,0:T(8,128)(2,1)S(1)}, bf16[32,16384]{1,0:T(8,128)(2,1)}, u32[]{:S(2)}) %copy-start.1) | copy-done | bytes 1048600
  36.2 0.0 copy-start.2
  36.2 0.0 copy-start.3
  36.2 0.0 copy-start.4
  36.2 0.0 copy-start.5
  36.2 11.2 %shard_map.71 = f32[8,16,128]{2,1,0:T(8,128)S(1)} custom-call(f32[8,8,128]{2,1,0:T(8,128)S(1)} %all-to-all-done.1.targets_ref.refs_0_, f32[8,160,128]{2,1,0:T(8,128)S(1)} %all_gather.6.got_ref, f32[16,128]{1,0:T(8,128)S(1)} %get-tuple-element.8.keep_ref, bf16[32,16384]{1,0:T(8,128)(2,1)S(1)} %copy-done.1, bf16[64,16384]{1,0:T(8,128)(2,1)S(1)} %get-tuple-element.10.cross_ref, ...), custom_call_target="tpu_custom_call" | custom-call | tf_op jit(solution)/shard_map/pallas_call | solution.py:381
  47.4 9.7 %all_to_all.21.refs_1_ = f32[8,16,128]{2,1,0:T(8,128)S(1)} all-to-all(f32[8,16,128]{2,1,0:T(8,128)S(1)} %shard_map.71), channel_id=1, replica_groups=mesh['z'=8,'x'=4,'c'=2,'aa'=8] {'z'}, dimensions={0} | all-to-all | bytes 131072 | tf_op jit(solution)/shard_map/all_to_all | solution.py:393
  57.1 0.1 shard_map.72
  57.2 17.3 %all_to_all.22 = f32[32,16,128]{2,1,0:T(8,128)S(1)} all-to-all(f32[32,16,128]{2,1,0:T(8,128)S(1)} %shard_map.72), channel_id=1, replica_groups=mesh['z'=8,'x'=4,'c'=2,'aa'=8] {'x','aa'}, dimensions={0} | all-to-all | bytes 524288 | tf_op jit(solution)/shard_map/all_to_all | solution.py:402
  74.5 6.1 %all_gather.7 = f32[64,16,128]{2,1,0:T(8,128)S(1)} all-gather(f32[32,16,128]{2,1,0:T(8,128)S(1)} %all_to_all.22), channel_id=1, replica_groups=mesh['z'=8,'x'=4,'c'=2,'aa'=8] {'c'}, dimensions={0}, use_global_device_ids=true | all-gather | bytes 786432 | tf_op jit(solution)/shard_map/all_gather | solution.py:403
  80.6 0.0 copy-done.2
  80.6 0.0 copy-done.3
  80.6 0.0 copy-done.4
  80.6 0.0 copy-done.5
  80.6 2.8 %shard_map.73 = (f32[12,1280]{1,0:T(8,128)}, f32[12,2048]{1,0:T(8,128)}) custom-call(f32[12,2048]{1,0:T(8,128)S(1)} %copy-done.2, s32[16,128]{1,0:T(8,128)S(1)} %bitcast.9, s32[16,128]{1,0:T(8,128)S(1)} %bitcast.11, s32[80,128]{1,0:T(8,128)S(1)} %bitcast.7, f32[8,8,16,128]{3,2,1,0:T(8,128)S(1)} %bitcast.5), custom_call_target="tpu_custom_call" | custom-call | tf_op jit(solution)/shard_map/pallas_call | solution.py:405
Async XLA Ops:
  21.3 13.7 %all-to-all-start.1 = ((f32[8,8,128]{2,1,0:T(8,128)}), f32[8,8,128]{2,1,0:T(8,128)S(1)}, u32[]{:S(2)}, u32[]{:S(2)}) async-start(f32[8,8,128]{2,1,0:T(8,128)} %get-tuple-element.7), calls=%async_computation.1 | async-start | bytes 65536 | tf_op jit(solution)/shard_map/all_to_all | solution.py:365
  28.9 1.0 %copy-start = (bf16[32,16384]{1,0:T(8,128)(2,1)}, bf16[32,16384]{1,0:T(8,128)(2,1)S(1)}, u32[]{:S(2)}) copy-start(bf16[32,16384]{1,0:T(8,128)(2,1)S(1)} %get-tuple-element.9.weight_ref) | copy-start | bytes 3145732
  35.0 1.2 %copy-start.1 = (bf16[32,16384]{1,0:T(8,128)(2,1)S(1)}, bf16[32,16384]{1,0:T(8,128)(2,1)}, u32[]{:S(2)}) copy-start(bf16[32,16384]{1,0:T(8,128)(2,1)} %copy-done) | copy-start | bytes 3145732
  36.2 44.4 %copy-start.2 = (f32[12,2048]{1,0:T(8,128)S(1)}, f32[12,2048]{1,0:T(8,128)}, u32[]{:S(2)}) copy-start(f32[12,2048]{1,0:T(8,128)} %state_ref.1) | copy-start | bytes 294916
  36.2 44.4 %copy-start.3 = (s32[10240]{0:T(1024)S(1)}, s32[10240]{0:T(1024)}, u32[]{:S(2)}) copy-start(s32[10240]{0:T(1024)} %param.9) | copy-start | bytes 122884
  36.2 44.4 %copy-start.4 = (s32[2048]{0:T(1024)S(1)}, s32[2048]{0:T(1024)}, u32[]{:S(2)}) copy-start(s32[2048]{0:T(1024)} %param.8) | copy-start | bytes 24580
  36.2 44.4 %copy-start.5 = (s32[2048]{0:T(1024)S(1)}, s32[2048]{0:T(1024)}, u32[]{:S(2)}) copy-start(s32[2048]{0:T(1024)} %param.7) | copy-start | bytes 24580

commit v5 on v3

--- a/solution.py
+++ b/solution.py
@@ -16,9 +16,11 @@
 MAIN, TAIL = 128, 32
 PER = MAIN + TAIL
 FIELD = 8 * TILES
-CHUNK = 512
+CHUNK = 1024
 ROWS = 16
 BLOCKS = PER // ROWS
+CROSSED = 8
+UNROLL = 8
 
 f32, bf16 = jnp.float32, jnp.bfloat16
 
@@ -128,7 +130,36 @@
     keep_ref[8:16, :] = jnp.broadcast_to(step, (8, 128))
 
 
-def force_kernel(targets_ref, got_ref, keep_ref, out_ref, seen_ref, weight_ref, sums_ref):
+def weight_rows(tile, row):
+    value = jnp.where(row < 6, tile * tile[6:7], jnp.where(row == 6, tile, 0.0))
+    first = value.astype(bf16).astype(f32)
+    rest = value - first
+    second = rest.astype(bf16).astype(f32)
+    return jnp.concatenate([first, second, rest - second, jnp.zeros_like(value)], axis=0).astype(bf16)
+
+
+def cross_rows(tile, row, center):
+    tile = tile - center
+    dot = jnp.sum(tile[0:3] * tile[3:6], axis=0, keepdims=True)
+    value = jnp.where(row < 6, tile, jnp.where(row == 6, 1.0, dot))
+    first = value.astype(bf16).astype(f32)
+    rest = value - first
+    second = rest.astype(bf16).astype(f32)
+    third = rest - second
+    return jnp.concatenate([first, second, first, second, third, first, third, second], axis=0).astype(bf16)
+
+
+def target_rows(pos, vel, center):
+    pos, vel = pos - center[0:3, 0:1], vel - center[3:6, 0:1]
+    value = jnp.concatenate([-vel, -pos, jnp.sum(pos * vel, axis=0, keepdims=True), jnp.ones_like(pos[0:1])], axis=0)
+    first = value.astype(bf16).astype(f32)
+    rest = value - first
+    second = rest.astype(bf16).astype(f32)
+    third = rest - second
+    return jnp.transpose(jnp.concatenate([first, first, second, second, first, third, second, third], axis=0)).astype(bf16)
+
+
+def force_kernel(targets_ref, got_ref, keep_ref, out_ref, seen_ref, left_ref, along_ref, sums_ref):
     target = targets_ref[0]
     for z in range(1, targets_ref.shape[0]):
         target = target + targets_ref[z]
@@ -139,42 +170,47 @@
             seen_ref[half * 3 + q, MAIN:PER, :] = jnp.broadcast_to(
                 columns[q * TAIL : (q + 1) * TAIL, half * 4 + 3 : half * 4 + 4], (TAIL, 128)
             )
-
     row = lax.broadcasted_iota(jnp.int32, (8, 128), 0)
-
-    def weigh(g, _):
-        for i in range(TILES):
-            tile = got_ref[g, i * 8 : (i + 1) * 8, :]
-            mass = tile[6:7]
-            value = jnp.where(row < 6, tile * mass, jnp.where(row == 6, tile, 0.0))
-            first = value.astype(bf16).astype(f32)
-            rest = value - first
-            second = rest.astype(bf16).astype(f32)
-            rows = jnp.concatenate([first, second, rest - second, jnp.zeros_like(value)], axis=0).astype(bf16)
-            weight_ref[:, pl.ds(pl.multiple_of((g * TILES + i) * 128, 128), 128)] = rows
-        return 0
-
-    lax.fori_loop(0, GROUPS, weigh, 0)
+    center = jnp.broadcast_to(jnp.mean(got_ref[0, 0:8, :], axis=1, keepdims=True), (8, 128))
+    center = jnp.where(row < 6, center, 0.0)
+    left_ref[...] = target_rows(target[0:3], target[4:7], center)[0 : CROSSED * ROWS]
     sums_ref[...] = jnp.zeros_like(sums_ref)
 
-    def chunk(n, _):
-        g, part = n // (TILES * 128 // CHUNK), n % (TILES * 128 // CHUNK)
-        base = pl.multiple_of(part * (CHUNK // 16), 8)
-        across = CHUNK // 128
+    across = CHUNK // 128
+    chunks = GROUPS * TILES // across
+
+    def tiles_of(n):
+        g, part = n // (TILES // across), n % (TILES // across)
+        return g, pl.multiple_of(part * (CHUNK // 16), 8)
+
+    def cross(n, slot):
+        g, base = tiles_of(n)
+        right = [cross_rows(got_ref[g, pl.ds(base + j * 8, 8), :], row, center) for j in range(across)]
+        along_ref[slot] = jnp.dot(left_ref[...], jnp.concatenate(right, axis=1), preferred_element_type=f32)
+
+    def chunk(n, slot):
+        g, base = tiles_of(n)
         star = [
             jnp.concatenate(
                 [jnp.broadcast_to(got_ref[g, pl.ds(base + j * 8 + q, 1), :], (ROWS, 128)) for j in range(across)], axis=1
             )
             for q in range(6)
         ]
-        weight = weight_ref[:, pl.ds(pl.multiple_of(n * CHUNK, CHUNK), CHUNK)]
+        weight = jnp.concatenate(
+            [weight_rows(got_ref[g, pl.ds(base + j * 8, 8), :], row) for j in range(across)], axis=1
+        )
         values = []
         for b in range(BLOCKS):
             r = slice(b * ROWS, (b + 1) * ROWS)
-            seen = [jnp.concatenate([seen_ref[q, r, :]] * across, axis=1) for q in range(6)]
-            dx, dy, dz, wx, wy, wz = [star[q] - seen[q] for q in range(6)]
+            needed = 3 if b < CROSSED else 6
+            apart = [star[q] - jnp.concatenate([seen_ref[q, r, :]] * across, axis=1) for q in range(needed)]
+            dx, dy, dz = apart[0:3]
             total = (dx * dx + EPS2) + dy * dy + dz * dz
-            along = dx * wx + dy * wy + dz * wz
+            if b < CROSSED:
+                along = along_ref[slot, r, :]
+            else:
+                wx, wy, wz = apart[3:6]
+                along = dx * wx + dy * wy + dz * wz
             inverse = lax.rsqrt(total)
             square = inverse * inverse
             cube = square * inverse
@@ -189,9 +225,16 @@
                 sums_ref[:, end - right.shape[0] : end] += lax.dot_general(
                     weight, right, (((1,), (1,)), ((), ())), preferred_element_type=f32
                 )
+
+    cross(0, 0)
+
+    def body(n, _):
+        for u in range(UNROLL):
+            cross(jnp.minimum(n * UNROLL + u + 1, chunks - 1), (u + 1) % 2)
+            chunk(n * UNROLL + u, u % 2)
         return 0
 
-    lax.fori_loop(0, GROUPS * TILES * 128 // CHUNK, chunk, 0, unroll=4)
+    lax.fori_loop(0, chunks // UNROLL, body, 0)
     sums = jnp.transpose(sums_ref[...])
 
     def columns_of(part):
@@ -344,7 +387,8 @@
         out_specs=vmem(1)[0],
         scratch_shapes=[
             pltpu.VMEM((6, PER, 128), f32),
-            pltpu.VMEM((32, GROUPS * TILES * 128), bf16),
+            pltpu.VMEM((CROSSED * ROWS, 64), bf16),
+            pltpu.VMEM((2, CROSSED * ROWS, CHUNK), f32),
             pltpu.VMEM((32, 4 * PER), f32),
         ],
         compiler_params=params(),

time: 82.6 us -> 79.8 us (0.966)
  Pallas kernels: 16.8 us -> 13.9 us
    pallas_call x1, Pallas kernels: 12 us -> 9.18 us  [per_device(): pl.pallas_call(force_kernel, out_shape=jax.ShapeDtypeStruct((z_count, 16,...]
where the time goes in v5:
time: 79.8 us; the launch traced here: 79.5 us
  blocking collectives  64.9 us (81%)
  Pallas kernels  13.9 us (17%)
    all_to_all x1, blocking collectives, per_device(): updates = lax.all_to_all(updates, ('x', 'aa'), 0, 0, tiled=True)  17.3 us
    all_to_all x1, blocking collectives, per_device(): targets = lax.all_to_all(targets, 'z', 0, 0, tiled=True)  13.5 us
    all_to_all x1, blocking collectives, per_device(): got = lax.all_to_all(message, 'x', 0, 0, tiled=True)  10.5 us
    all_to_all x1, blocking collectives, per_device(): partial = lax.all_to_all(partial, 'z', 0, 0, tiled=True)  9.71 us
    pallas_call x1, Pallas kernels, per_device(): pl.pallas_call(force_kernel, out_shape=jax.ShapeDtypeStruct((z_count, 16,...  9.18 us
    all_gather x1, blocking collectives, per_device(): got = lax.all_gather(got, 'c', tiled=True)  7.65 us
    all_gather x1, blocking collectives, per_device(): lax.all_gather(updates, 'c', tiled=True).reshape(GROUPS, y_count, 16, 128)  6.28 us
    pallas_call x1, Pallas kernels, per_device(): pl.pallas_call(store_kernel, out_shape=[jax.ShapeDtypeStruct((12, 1280),...  2.79 us

profile of v5, /device:TPU:1, one launch (start us, length us, event | category | flops | bytes accessed | tf_op | source)
XLA Modules:
  0.0 79.5 jit_solution(16802392945926702258)
XLA Ops:
  0.6 1.8 %shard_map.68 = f32[4,160,128]{2,1,0:T(8,128)S(1)} custom-call(f32[12,2048]{1,0:T(8,128)} %state_ref.1, f32[16,128]{1,0:T(8,128)} %bitcast.12, s32[16,128]{1,0:T(8,128)} %bitcast.8, s32[16,128]{1,0:T(8,128)} %bitcast.10, s32[80,128]{1,0:T(8,128)} %bitcast.6), custom_call_target="tpu_custom_call" | custom-call | tf_op jit(solution)/shard_map/pallas_call | solution.py:361
  2.5 10.5 %all_to_all.20 = f32[4,160,128]{2,1,0:T(8,128)S(1)} all-to-all(f32[4,160,128]{2,1,0:T(8,128)S(1)} %shard_map.68), channel_id=1, replica_groups=mesh['z'=8,'x'=4,'c'=2,'aa'=8] {'x'}, dimensions={0} | all-to-all | bytes 655360 | tf_op jit(solution)/shard_map/all_to_all | solution.py:371
  13.0 7.6 %all_gather.6.got_ref = f32[8,160,128]{2,1,0:T(8,128)S(1)} all-gather(f32[4,160,128]{2,1,0:T(8,128)S(1)} %all_to_all.20), channel_id=1, replica_groups=mesh['z'=8,'x'=4,'c'=2,'aa'=8] {'c'}, dimensions={0}, use_global_device_ids=true | all-gather | bytes 983040 | tf_op jit(solution)/shard_map/all_gather | solution.py:372
  20.7 13.5 %all_to_all.21.targets_ref.refs_0_ = f32[8,8,128]{2,1,0:T(8,128)S(1)} all-to-all(f32[8,8,128]{2,1,0:T(8,128)S(1)} %get-tuple-element.4), channel_id=1, replica_groups=mesh['z'=8,'x'=4,'c'=2,'aa'=8] {'z'}, dimensions={0} | all-to-all | bytes 65536 | tf_op jit(solution)/shard_map/all_to_all | solution.py:381
  34.1 9.2 %shard_map.70 = f32[8,16,128]{2,1,0:T(8,128)S(1)} custom-call(f32[8,8,128]{2,1,0:T(8,128)S(1)} %all_to_all.21.targets_ref.refs_0_, f32[8,160,128]{2,1,0:T(8,128)S(1)} %all_gather.6.got_ref, f32[16,128]{1,0:T(8,128)S(1)} %get-tuple-element.5.keep_ref), custom_call_target="tpu_custom_call" | custom-call | tf_op jit(solution)/shard_map/pallas_call | solution.py:383
  43.3 9.7 %all_to_all.22.refs_1_ = f32[8,16,128]{2,1,0:T(8,128)S(1)} all-to-all(f32[8,16,128]{2,1,0:T(8,128)S(1)} %shard_map.70), channel_id=1, replica_groups=mesh['z'=8,'x'=4,'c'=2,'aa'=8] {'z'}, dimensions={0} | all-to-all | bytes 131072 | tf_op jit(solution)/shard_map/all_to_all | solution.py:396
  53.0 0.1 shard_map.71
  53.1 17.3 %all_to_all.23 = f32[32,16,128]{2,1,0:T(8,128)S(1)} all-to-all(f32[32,16,128]{2,1,0:T(8,128)S(1)} %shard_map.71), channel_id=1, replica_groups=mesh['z'=8,'x'=4,'c'=2,'aa'=8] {'x','aa'}, dimensions={0} | all-to-all | bytes 524288 | tf_op jit(solution)/shard_map/all_to_all | solution.py:405
  70.4 0.0 copy-start
  70.4 0.0 copy-start.1
  70.4 0.0 copy-start.2
  70.4 0.0 copy-start.3
  70.4 6.3 %all_gather.7 = f32[64,16,128]{2,1,0:T(8,128)S(1)} all-gather(f32[32,16,128]{2,1,0:T(8,128)S(1)} %all_to_all.23), channel_id=1, replica_groups=mesh['z'=8,'x'=4,'c'=2,'aa'=8] {'c'}, dimensions={0}, use_global_device_ids=true | all-gather | bytes 786432 | tf_op jit(solution)/shard_map/all_gather | solution.py:406
  76.7 0.0 copy-done
  76.7 0.0 copy-done.1
  76.7 0.0 copy-done.2
  76.7 0.0 copy-done.3
  76.7 2.8 %shard_map.72 = (f32[12,1280]{1,0:T(8,128)}, f32[12,2048]{1,0:T(8,128)}) custom-call(f32[12,2048]{1,0:T(8,128)S(1)} %copy-done, s32[16,128]{1,0:T(8,128)S(1)} %bitcast.9, s32[16,128]{1,0:T(8,128)S(1)} %bitcast.11, s32[80,128]{1,0:T(8,128)S(1)} %bitcast.7, f32[8,8,16,128]{3,2,1,0:T(8,128)S(1)} %bitcast.5), custom_call_target="tpu_custom_call" | custom-call | tf_op jit(solution)/shard_map/pallas_call | solution.py:408
  (1 shorter events, 0.0 us)
Async XLA Ops:
  70.4 6.3 %copy-start = (f32[12,2048]{1,0:T(8,128)S(1)}, f32[12,2048]{1,0:T(8,128)}, u32[]{:S(2)}) copy-start(f32[12,2048]{1,0:T(8,128)} %state_ref.1) | copy-start | bytes 294916
  70.4 6.3 %copy-start.1 = (s32[10240]{0:T(1024)S(1)}, s32[10240]{0:T(1024)}, u32[]{:S(2)}) copy-start(s32[10240]{0:T(1024)} %param.9) | copy-start | bytes 122884
  70.4 6.3 %copy-start.2 = (s32[2048]{0:T(1024)S(1)}, s32[2048]{0:T(1024)}, u32[]{:S(2)}) copy-start(s32[2048]{0:T(1024)} %param.8) | copy-start | bytes 24580
  70.4 6.3 %copy-start.3 = (s32[2048]{0:T(1024)S(1)}, s32[2048]{0:T(1024)}, u32[]{:S(2)}) copy-start(s32[2048]{0:T(1024)} %param.7) | copy-start | bytes 24580

commit v6 on v5

--- a/solution.py
+++ b/solution.py
@@ -19,7 +19,7 @@
 CHUNK = 1024
 ROWS = 16
 BLOCKS = PER // ROWS
-CROSSED = 8
+CROSSED = MAIN // ROWS
 UNROLL = 8
 
 f32, bf16 = jnp.float32, jnp.bfloat16
@@ -71,15 +71,22 @@
 
 
 def pick_kernel(*refs):
-    given, msg_ref, table_ref, held, sems = refs[:5], refs[5], refs[6], refs[7:12], refs[12]
+    given, msg_ref, table_ref, chosen_ref, held, sems = refs[:5], refs[5], refs[6], refs[7], refs[8:13], refs[13]
     copies = [pltpu.make_async_copy(a, b, sems.at[n]) for n, (a, b) in enumerate(zip(given, held))]
     for copy in copies:
         copy.start()
-    for copy in copies:
-        copy.wait()
-    state_ref, mass_ref, ticks_ref, levels_ref, active_ref = held
+    active_ref, state_ref, mass_ref, ticks_ref, levels_ref = held
     start = first_star()
     block = lax.axis_index("aa") * 10
+    copies[0].wait()
+    rows = lax.broadcasted_iota(jnp.int32, (256, 128), 0)
+    highs = []
+    for k in range(10):
+        local = active_ref[pl.ds(block + k, 1), :] - start
+        highs.append(jnp.right_shift(local, 8))
+        chosen_ref[:, k * 128 : (k + 1) * 128] = jnp.where(rows == jnp.bitwise_and(local, 255), 1.0, 0.0).astype(bf16)
+    for copy in copies[1:]:
+        copy.wait()
     zero = jnp.zeros((1, 128), f32)
     for i in range(TILES):
         s = state_ref[:, i * 128 : (i + 1) * 128]
@@ -89,23 +96,22 @@
         field = jnp.concatenate([pos, vel, mass_ref[i : i + 1, :], zero], axis=0)
         both = jnp.concatenate([field, s[6:12], step, zero], axis=0)
         for n, part in enumerate(split3(both)):
-            table_ref[n * 256 + i * 16 : n * 256 + (i + 1) * 16, :] = part
+            row = n * 128 + i // 2 * 16
+            table_ref[row : row + 16, i % 2 * 128 : (i % 2 + 1) * 128] = part
         for x in range(X):
             msg_ref[x, i * 8 : (i + 1) * 8, :] = field
-    rows = lax.broadcasted_iota(jnp.int32, (128, 128), 0)
     picks = []
-    for k in range(10):
-        local = active_ref[pl.ds(block + k, 1), :] - start
-        high = jnp.broadcast_to(jnp.right_shift(local, 7), (16, 128))
-        low = jnp.bitwise_and(local, 127)
-        chosen = jnp.where(rows == low, 1.0, 0.0).astype(bf16)
-        found = jnp.dot(table_ref[...], chosen, preferred_element_type=f32)
-        pick = jnp.zeros((16, 128), f32)
-        for h in range(TILES):
-            r = slice(h * 16, (h + 1) * 16)
-            value = (found[0:256][r] + found[256:512][r]) + found[512:768][r]
-            pick = jnp.where(high == h, value, pick)
-        picks.append(pick)
+    for pair in range(5):
+        found = jnp.dot(
+            table_ref[...], chosen_ref[:, pair * 256 : (pair + 1) * 256], preferred_element_type=f32
+        )
+        for k in range(2):
+            high = jnp.broadcast_to(highs[2 * pair + k], (16, 128))
+            pick = jnp.zeros((16, 128), f32)
+            for h in range(TILES // 2):
+                r = [found[n * 128 + h * 16 : n * 128 + (h + 1) * 16, k * 128 : (k + 1) * 128] for n in range(3)]
+                pick = jnp.where(high == h, (r[0] + r[1]) + r[2], pick)
+            picks.append(pick)
     for g in range(GROUPS):
         main = picks[g]
         tail = picks[8 + g // 4][:, (g % 4) * TAIL : (g % 4 + 1) * TAIL]
@@ -164,16 +170,16 @@
     for z in range(1, targets_ref.shape[0]):
         target = target + targets_ref[z]
     columns = jnp.transpose(target)
-    for half in range(2):
-        for q in range(3):
-            seen_ref[half * 3 + q, 0:MAIN, :] = jnp.broadcast_to(columns[:, half * 4 + q : half * 4 + q + 1], (MAIN, 128))
+    for q in range(3):
+        seen_ref[q, 0:MAIN, :] = jnp.broadcast_to(columns[:, q : q + 1], (MAIN, 128))
+        for half in range(2):
             seen_ref[half * 3 + q, MAIN:PER, :] = jnp.broadcast_to(
                 columns[q * TAIL : (q + 1) * TAIL, half * 4 + 3 : half * 4 + 4], (TAIL, 128)
             )
     row = lax.broadcasted_iota(jnp.int32, (8, 128), 0)
     center = jnp.broadcast_to(jnp.mean(got_ref[0, 0:8, :], axis=1, keepdims=True), (8, 128))
     center = jnp.where(row < 6, center, 0.0)
-    left_ref[...] = target_rows(target[0:3], target[4:7], center)[0 : CROSSED * ROWS]
+    left_ref[...] = target_rows(target[0:3], target[4:7], center)
     sums_ref[...] = jnp.zeros_like(sums_ref)
 
     across = CHUNK // 128
@@ -316,7 +322,7 @@
     one = jnp.ones((1, 128), f32)
     sums_ref[...] = jnp.zeros_like(sums_ref)
 
-    def block(y, _):
+    def block(y):
         tiles = [jnp.where(row8 == 3, 1.0, got_ref[c * X + x, y, 0:8, :]) for c in range(C) for x in range(X)]
         for c in range(C):
             tiles.append(jnp.concatenate([tails(c, y, 3), one, tails(c, y, 7), one], axis=0))
@@ -335,9 +341,9 @@
             preferred_element_type=f32,
         )
         sums_ref[...] += total
-        return 0
-
-    lax.fori_loop(0, got_ref.shape[1], block, 0, unroll=4)
+
+    for y in range(got_ref.shape[1]):
+        block(y)
 
     for i in range(TILES):
         lanes = slice(i * 128, (i + 1) * 128)
@@ -363,11 +369,11 @@
         out_shape=jax.ShapeDtypeStruct((X, FIELD + 16 * C, 128), f32),
         in_specs=[pl.BlockSpec(memory_space=pltpu.HBM)] * 5,
         out_specs=vmem(1)[0],
-        scratch_shapes=[pltpu.VMEM((768, 128), bf16)]
-        + [pltpu.VMEM(a.shape, a.dtype) for a in (state, mass, ticks, levels, active)]
+        scratch_shapes=[pltpu.VMEM((384, 256), bf16), pltpu.VMEM((256, 1280), bf16)]
+        + [pltpu.VMEM(a.shape, a.dtype) for a in (active, state, mass, ticks, levels)]
         + [pltpu.SemaphoreType.DMA((5,))],
         compiler_params=params(),
-    )(*[pltpu.with_memory_space_constraint(a, pltpu.HBM) for a in (state, mass, ticks, levels, active)])
+    )(*[pltpu.with_memory_space_constraint(a, pltpu.HBM) for a in (active, state, mass, ticks, levels)])
     got = lax.all_to_all(message, "x", 0, 0, tiled=True)
     got = lax.all_gather(got, "c", tiled=True)
 

time: 79.8 us -> 79.2 us (level)
  no operation moved by 1% of the time
where the time goes in v6:
time: 79.2 us; the launch traced here: 78.9 us
  blocking collectives  64.9 us (82%)
  Pallas kernels  13.3 us (17%)
    all_to_all x1, blocking collectives, per_device(): updates = lax.all_to_all(updates, ('x', 'aa'), 0, 0, tiled=True)  17.3 us
    all_to_all x1, blocking collectives, per_device(): targets = lax.all_to_all(targets, 'z', 0, 0, tiled=True)  13.5 us
    all_to_all x1, blocking collectives, per_device(): got = lax.all_to_all(message, 'x', 0, 0, tiled=True)  10.5 us
    all_to_all x1, blocking collectives, per_device(): partial = lax.all_to_all(partial, 'z', 0, 0, tiled=True)  9.7 us
    pallas_call x1, Pallas kernels, per_device(): pl.pallas_call(force_kernel, out_shape=jax.ShapeDtypeStruct((z_count, 16,...  9.16 us
    all_gather x1, blocking collectives, per_device(): got = lax.all_gather(got, 'c', tiled=True)  7.65 us
    all_gather x1, blocking collectives, per_device(): lax.all_gather(updates, 'c', tiled=True).reshape(GROUPS, y_count, 16, 128)  6.28 us
    pallas_call x1, Pallas kernels, per_device(): pl.pallas_call(store_kernel, out_shape=[jax.ShapeDtypeStruct((12, 1280),...  2.45 us

profile of v6, /device:TPU:1, one launch (start us, length us, event | category | flops | bytes accessed | tf_op | source)
XLA Modules:
  0.0 78.9 jit_solution(11901291674845536831)
XLA Ops:
  0.6 1.6 %shard_map.68 = f32[4,160,128]{2,1,0:T(8,128)S(1)} custom-call(s32[80,128]{1,0:T(8,128)} %bitcast.6, f32[12,2048]{1,0:T(8,128)} %state_ref.1, f32[16,128]{1,0:T(8,128)} %bitcast.12, s32[16,128]{1,0:T(8,128)} %bitcast.8, s32[16,128]{1,0:T(8,128)} %bitcast.10), custom_call_target="tpu_custom_call" | custom-call | tf_op jit(solution)/shard_map/pallas_call | solution.py:367
  2.2 10.5 %all_to_all.20 = f32[4,160,128]{2,1,0:T(8,128)S(1)} all-to-all(f32[4,160,128]{2,1,0:T(8,128)S(1)} %shard_map.68), channel_id=1, replica_groups=mesh['z'=8,'x'=4,'c'=2,'aa'=8] {'x'}, dimensions={0} | all-to-all | bytes 655360 | tf_op jit(solution)/shard_map/all_to_all | solution.py:377
  12.7 7.6 %all_gather.6.got_ref = f32[8,160,128]{2,1,0:T(8,128)S(1)} all-gather(f32[4,160,128]{2,1,0:T(8,128)S(1)} %all_to_all.20), channel_id=1, replica_groups=mesh['z'=8,'x'=4,'c'=2,'aa'=8] {'c'}, dimensions={0}, use_global_device_ids=true | all-gather | bytes 983040 | tf_op jit(solution)/shard_map/all_gather | solution.py:378
  20.4 13.5 %all_to_all.21.targets_ref.refs_0_ = f32[8,8,128]{2,1,0:T(8,128)S(1)} all-to-all(f32[8,8,128]{2,1,0:T(8,128)S(1)} %get-tuple-element.4), channel_id=1, replica_groups=mesh['z'=8,'x'=4,'c'=2,'aa'=8] {'z'}, dimensions={0} | all-to-all | bytes 65536 | tf_op jit(solution)/shard_map/all_to_all | solution.py:387
  33.9 9.2 %shard_map.70 = f32[8,16,128]{2,1,0:T(8,128)S(1)} custom-call(f32[8,8,128]{2,1,0:T(8,128)S(1)} %all_to_all.21.targets_ref.refs_0_, f32[8,160,128]{2,1,0:T(8,128)S(1)} %all_gather.6.got_ref, f32[16,128]{1,0:T(8,128)S(1)} %get-tuple-element.5.keep_ref), custom_call_target="tpu_custom_call" | custom-call | tf_op jit(solution)/shard_map/pallas_call | solution.py:389
  43.0 9.7 %all_to_all.22.refs_1_ = f32[8,16,128]{2,1,0:T(8,128)S(1)} all-to-all(f32[8,16,128]{2,1,0:T(8,128)S(1)} %shard_map.70), channel_id=1, replica_groups=mesh['z'=8,'x'=4,'c'=2,'aa'=8] {'z'}, dimensions={0} | all-to-all | bytes 131072 | tf_op jit(solution)/shard_map/all_to_all | solution.py:402
  52.7 0.1 shard_map.71
  52.8 17.3 %all_to_all.23 = f32[32,16,128]{2,1,0:T(8,128)S(1)} all-to-all(f32[32,16,128]{2,1,0:T(8,128)S(1)} %shard_map.71), channel_id=1, replica_groups=mesh['z'=8,'x'=4,'c'=2,'aa'=8] {'x','aa'}, dimensions={0} | all-to-all | bytes 524288 | tf_op jit(solution)/shard_map/all_to_all | solution.py:411
  70.2 0.0 copy-start
  70.2 0.0 copy-start.1
  70.2 0.0 copy-start.2
  70.2 0.0 copy-start.3
  70.2 6.3 %all_gather.7 = f32[64,16,128]{2,1,0:T(8,128)S(1)} all-gather(f32[32,16,128]{2,1,0:T(8,128)S(1)} %all_to_all.23), channel_id=1, replica_groups=mesh['z'=8,'x'=4,'c'=2,'aa'=8] {'c'}, dimensions={0}, use_global_device_ids=true | all-gather | bytes 786432 | tf_op jit(solution)/shard_map/all_gather | solution.py:412
  76.4 0.0 copy-done
  76.4 0.0 copy-done.1
  76.4 0.0 copy-done.2
  76.5 0.0 copy-done.3
  76.5 2.5 %shard_map.72 = (f32[12,1280]{1,0:T(8,128)}, f32[12,2048]{1,0:T(8,128)}) custom-call(f32[12,2048]{1,0:T(8,128)S(1)} %copy-done, s32[16,128]{1,0:T(8,128)S(1)} %bitcast.9, s32[16,128]{1,0:T(8,128)S(1)} %bitcast.11, s32[80,128]{1,0:T(8,128)S(1)} %bitcast.7, f32[8,8,16,128]{3,2,1,0:T(8,128)S(1)} %bitcast.5), custom_call_target="tpu_custom_call" | custom-call | tf_op jit(solution)/shard_map/pallas_call | solution.py:414
  (1 shorter events, 0.0 us)
Async XLA Ops:
  70.2 6.3 %copy-start = (f32[12,2048]{1,0:T(8,128)S(1)}, f32[12,2048]{1,0:T(8,128)}, u32[]{:S(2)}) copy-start(f32[12,2048]{1,0:T(8,128)} %state_ref.1) | copy-start | bytes 294916
  70.2 6.3 %copy-start.1 = (s32[10240]{0:T(1024)S(1)}, s32[10240]{0:T(1024)}, u32[]{:S(2)}) copy-start(s32[10240]{0:T(1024)} %param.9) | copy-start | bytes 122884
  70.2 6.3 %copy-start.2 = (s32[2048]{0:T(1024)S(1)}, s32[2048]{0:T(1024)}, u32[]{:S(2)}) copy-start(s32[2048]{0:T(1024)} %param.8) | copy-start | bytes 24580
  70.2 6.3 %copy-start.3 = (s32[2048]{0:T(1024)S(1)}, s32[2048]{0:T(1024)}, u32[]{:S(2)}) copy-start(s32[2048]{0:T(1024)} %param.7) | copy-start | bytes 24580

commit v7 on v6

--- a/solution.py
+++ b/solution.py
@@ -136,8 +136,8 @@
     keep_ref[8:16, :] = jnp.broadcast_to(step, (8, 128))
 
 
-def weight_rows(tile, row):
-    value = jnp.where(row < 6, tile * tile[6:7], jnp.where(row == 6, tile, 0.0))
+def weight_rows(tile, row, center):
+    value = (jnp.where(row < 6, tile, 1.0) - center) * tile[6:7]
     first = value.astype(bf16).astype(f32)
     rest = value - first
     second = rest.astype(bf16).astype(f32)
@@ -145,9 +145,9 @@
 
 
 def cross_rows(tile, row, center):
-    tile = tile - center
+    tile = jnp.where(row < 6, tile, 1.0) - center
     dot = jnp.sum(tile[0:3] * tile[3:6], axis=0, keepdims=True)
-    value = jnp.where(row < 6, tile, jnp.where(row == 6, 1.0, dot))
+    value = jnp.where(row == 7, dot, tile)
     first = value.astype(bf16).astype(f32)
     rest = value - first
     second = rest.astype(bf16).astype(f32)
@@ -203,7 +203,7 @@
             for q in range(6)
         ]
         weight = jnp.concatenate(
-            [weight_rows(got_ref[g, pl.ds(base + j * 8, 8), :], row) for j in range(across)], axis=1
+            [weight_rows(got_ref[g, pl.ds(base + j * 8, 8), :], row, center) for j in range(across)], axis=1
         )
         values = []
         for b in range(BLOCKS):
@@ -266,8 +266,10 @@
     main, tail = columns_of(2)
     rate_pos = pack(main[0:3], tail[0:3])
     rate_one = pack(three(main[6:7]), three(tail[6:7]))
-    acc = cube_pos - target[0:4] * cube_one
-    jerk = (cube_vel - target[4:8] * cube_one) - 3.0 * (rate_pos - target[0:4] * rate_one)
+    pos = target[0:4] - pack(center[0:3], center[0:3, 0:TAIL])
+    vel = target[4:8] - pack(center[3:6], center[3:6, 0:TAIL])
+    acc = cube_pos - pos * cube_one
+    jerk = (cube_vel - vel * cube_one) - 3.0 * (rate_pos - pos * rate_one)
     last = jnp.concatenate([acc[3:4, 0:96], keep_ref[8:9, 0:TAIL]], axis=1)
     forces = jnp.concatenate([acc[0:3], last, jerk], axis=0)
     for z in range(out_ref.shape[0]):

time: 79.2 us -> 79.2 us (level)
  no operation moved by 1% of the time
where the time goes in v7:
time: 79.2 us; the launch traced here: 78.9 us
  blocking collectives  64.9 us (82%)
  Pallas kernels  13.3 us (17%)
    all_to_all x1, blocking collectives, per_device(): updates = lax.all_to_all(updates, ('x', 'aa'), 0, 0, tiled=True)  17.3 us
    all_to_all x1, blocking collectives, per_device(): targets = lax.all_to_all(targets, 'z', 0, 0, tiled=True)  13.5 us
    all_to_all x1, blocking collectives, per_device(): got = lax.all_to_all(message, 'x', 0, 0, tiled=True)  10.5 us
    all_to_all x1, blocking collectives, per_device(): partial = lax.all_to_all(partial, 'z', 0, 0, tiled=True)  9.7 us
    pallas_call x1, Pallas kernels, per_device(): pl.pallas_call(force_kernel, out_shape=jax.ShapeDtypeStruct((z_count, 16,...  9.16 us
    all_gather x1, blocking collectives, per_device(): got = lax.all_gather(got, 'c', tiled=True)  7.65 us
    all_gather x1, blocking collectives, per_device(): lax.all_gather(updates, 'c', tiled=True).reshape(GROUPS, y_count, 16, 128)  6.27 us
    pallas_call x1, Pallas kernels, per_device(): pl.pallas_call(store_kernel, out_shape=[jax.ShapeDtypeStruct((12, 1280),...  2.45 us

profile of v7, /device:TPU:1, one launch (start us, length us, event | category | flops | bytes accessed | tf_op | source)
XLA Modules:
  0.0 78.9 jit_solution(18299405128310204987)
XLA Ops:
  0.6 1.6 %shard_map.68 = f32[4,160,128]{2,1,0:T(8,128)S(1)} custom-call(s32[80,128]{1,0:T(8,128)} %bitcast.6, f32[12,2048]{1,0:T(8,128)} %state_ref.1, f32[16,128]{1,0:T(8,128)} %bitcast.12, s32[16,128]{1,0:T(8,128)} %bitcast.8, s32[16,128]{1,0:T(8,128)} %bitcast.10), custom_call_target="tpu_custom_call" | custom-call | tf_op jit(solution)/shard_map/pallas_call | solution.py:369
  2.2 10.5 %all_to_all.20 = f32[4,160,128]{2,1,0:T(8,128)S(1)} all-to-all(f32[4,160,128]{2,1,0:T(8,128)S(1)} %shard_map.68), channel_id=1, replica_groups=mesh['z'=8,'x'=4,'c'=2,'aa'=8] {'x'}, dimensions={0} | all-to-all | bytes 655360 | tf_op jit(solution)/shard_map/all_to_all | solution.py:379
  12.7 7.6 %all_gather.6.got_ref = f32[8,160,128]{2,1,0:T(8,128)S(1)} all-gather(f32[4,160,128]{2,1,0:T(8,128)S(1)} %all_to_all.20), channel_id=1, replica_groups=mesh['z'=8,'x'=4,'c'=2,'aa'=8] {'c'}, dimensions={0}, use_global_device_ids=true | all-gather | bytes 983040 | tf_op jit(solution)/shard_map/all_gather | solution.py:380
  20.4 13.5 %all_to_all.21.targets_ref.refs_0_ = f32[8,8,128]{2,1,0:T(8,128)S(1)} all-to-all(f32[8,8,128]{2,1,0:T(8,128)S(1)} %get-tuple-element.4), channel_id=1, replica_groups=mesh['z'=8,'x'=4,'c'=2,'aa'=8] {'z'}, dimensions={0} | all-to-all | bytes 65536 | tf_op jit(solution)/shard_map/all_to_all | solution.py:389
  33.9 9.2 %shard_map.70 = f32[8,16,128]{2,1,0:T(8,128)S(1)} custom-call(f32[8,8,128]{2,1,0:T(8,128)S(1)} %all_to_all.21.targets_ref.refs_0_, f32[8,160,128]{2,1,0:T(8,128)S(1)} %all_gather.6.got_ref, f32[16,128]{1,0:T(8,128)S(1)} %get-tuple-element.5.keep_ref), custom_call_target="tpu_custom_call" | custom-call | tf_op jit(solution)/shard_map/pallas_call | solution.py:391
  43.0 9.7 %all_to_all.22.refs_1_ = f32[8,16,128]{2,1,0:T(8,128)S(1)} all-to-all(f32[8,16,128]{2,1,0:T(8,128)S(1)} %shard_map.70), channel_id=1, replica_groups=mesh['z'=8,'x'=4,'c'=2,'aa'=8] {'z'}, dimensions={0} | all-to-all | bytes 131072 | tf_op jit(solution)/shard_map/all_to_all | solution.py:404
  52.7 0.1 shard_map.71
  52.9 17.3 %all_to_all.23 = f32[32,16,128]{2,1,0:T(8,128)S(1)} all-to-all(f32[32,16,128]{2,1,0:T(8,128)S(1)} %shard_map.71), channel_id=1, replica_groups=mesh['z'=8,'x'=4,'c'=2,'aa'=8] {'x','aa'}, dimensions={0} | all-to-all | bytes 524288 | tf_op jit(solution)/shard_map/all_to_all | solution.py:413
  70.2 0.0 copy-start
  70.2 0.0 copy-start.1
  70.2 0.0 copy-start.2
  70.2 0.0 copy-start.3
  70.2 6.3 %all_gather.7 = f32[64,16,128]{2,1,0:T(8,128)S(1)} all-gather(f32[32,16,128]{2,1,0:T(8,128)S(1)} %all_to_all.23), channel_id=1, replica_groups=mesh['z'=8,'x'=4,'c'=2,'aa'=8] {'c'}, dimensions={0}, use_global_device_ids=true | all-gather | bytes 786432 | tf_op jit(solution)/shard_map/all_gather | solution.py:414
  76.4 0.0 copy-done
  76.4 0.0 copy-done.1
  76.4 0.0 copy-done.2
  76.5 0.0 copy-done.3
  76.5 2.5 %shard_map.72 = (f32[12,1280]{1,0:T(8,128)}, f32[12,2048]{1,0:T(8,128)}) custom-call(f32[12,2048]{1,0:T(8,128)S(1)} %copy-done, s32[16,128]{1,0:T(8,128)S(1)} %bitcast.9, s32[16,128]{1,0:T(8,128)S(1)} %bitcast.11, s32[80,128]{1,0:T(8,128)S(1)} %bitcast.7, f32[8,8,16,128]{3,2,1,0:T(8,128)S(1)} %bitcast.5), custom_call_target="tpu_custom_call" | custom-call | tf_op jit(solution)/shard_map/pallas_call | solution.py:416
  (1 shorter events, 0.0 us)
Async XLA Ops:
  70.2 6.3 %copy-start = (f32[12,2048]{1,0:T(8,128)S(1)}, f32[12,2048]{1,0:T(8,128)}, u32[]{:S(2)}) copy-start(f32[12,2048]{1,0:T(8,128)} %state_ref.1) | copy-start | bytes 294916
  70.2 6.3 %copy-start.1 = (s32[10240]{0:T(1024)S(1)}, s32[10240]{0:T(1024)}, u32[]{:S(2)}) copy-start(s32[10240]{0:T(1024)} %param.9) | copy-start | bytes 122884
  70.2 6.3 %copy-start.2 = (s32[2048]{0:T(1024)S(1)}, s32[2048]{0:T(1024)}, u32[]{:S(2)}) copy-start(s32[2048]{0:T(1024)} %param.8) | copy-start | bytes 24580
  70.2 6.3 %copy-start.3 = (s32[2048]{0:T(1024)S(1)}, s32[2048]{0:T(1024)}, u32[]{:S(2)}) copy-start(s32[2048]{0:T(1024)} %param.7) | copy-start | bytes 24580

commit v8 on v7

--- a/solution.py
+++ b/solution.py
@@ -320,7 +320,8 @@
         new_active_ref[9:12, lanes] = tails(c, mine, 7)
 
     row8 = lax.broadcasted_iota(jnp.int32, (8, 128), 0)
-    rows = lax.broadcasted_iota(jnp.int32, (128, 128), 0)
+    rows = lax.broadcasted_iota(jnp.int32, (128, 128), 0).astype(f32).astype(bf16)
+    nothing, unit = jnp.zeros((16, 128), bf16), jnp.ones((128, 128), bf16)
     one = jnp.ones((1, 128), f32)
     sums_ref[...] = jnp.zeros_like(sums_ref)
 
@@ -331,11 +332,12 @@
         lefts, lows = [], []
         for k, tile in enumerate(tiles):
             local = active_ref[pl.ds(y * 10 + k, 1), :] - start
-            high = jnp.broadcast_to(jnp.right_shift(local, 7), (16, 128))
-            lows.append(jnp.where(rows == jnp.bitwise_and(local, 127), 1.0, 0.0).astype(bf16))
+            high = jnp.broadcast_to(jnp.right_shift(local, 7).astype(f32), (16, 128)).astype(bf16)
+            low = jnp.broadcast_to(jnp.bitwise_and(local, 127).astype(f32), (128, 128)).astype(bf16)
+            lows.append(jnp.where(rows == low, unit, jnp.zeros_like(unit)))
             first = tile.astype(bf16).astype(f32)
-            both = jnp.concatenate([first, tile - first], axis=0)
-            lefts.append(jnp.concatenate([jnp.where(high == h, both, 0.0).astype(bf16) for h in range(TILES)], axis=0))
+            both = jnp.concatenate([first, tile - first], axis=0).astype(bf16)
+            lefts.append(jnp.concatenate([jnp.where(high == h, both, nothing) for h in range(TILES)], axis=0))
         total = lax.dot_general(
             jnp.concatenate(lefts, axis=1),
             jnp.concatenate(lows, axis=1),

time: 79.2 us -> 79.1 us (level)
  no operation moved by 1% of the time
where the time goes in v8:
time: 79.1 us; the launch traced here: 78.8 us
  blocking collectives  64.9 us (82%)
  Pallas kernels  13.2 us (17%)
    all_to_all x1, blocking collectives, per_device(): updates = lax.all_to_all(updates, ('x', 'aa'), 0, 0, tiled=True)  17.3 us
    all_to_all x1, blocking collectives, per_device(): targets = lax.all_to_all(targets, 'z', 0, 0, tiled=True)  13.5 us
    all_to_all x1, blocking collectives, per_device(): got = lax.all_to_all(message, 'x', 0, 0, tiled=True)  10.5 us
    all_to_all x1, blocking collectives, per_device(): partial = lax.all_to_all(partial, 'z', 0, 0, tiled=True)  9.7 us
    pallas_call x1, Pallas kernels, per_device(): pl.pallas_call(force_kernel, out_shape=jax.ShapeDtypeStruct((z_count, 16,...  9.16 us
    all_gather x1, blocking collectives, per_device(): got = lax.all_gather(got, 'c', tiled=True)  7.65 us
    all_gather x1, blocking collectives, per_device(): lax.all_gather(updates, 'c', tiled=True).reshape(GROUPS, y_count, 16, 128)  6.27 us
    pallas_call x1, Pallas kernels, per_device(): pl.pallas_call(store_kernel, out_shape=[jax.ShapeDtypeStruct((12, 1280),...  2.34 us

profile of v8, /device:TPU:1, one launch (start us, length us, event | category | flops | bytes accessed | tf_op | source)
XLA Modules:
  0.0 78.8 jit_solution(15732039644353820594)
XLA Ops:
  0.6 1.6 %shard_map.68 = f32[4,160,128]{2,1,0:T(8,128)S(1)} custom-call(s32[80,128]{1,0:T(8,128)} %bitcast.6, f32[12,2048]{1,0:T(8,128)} %state_ref.1, f32[16,128]{1,0:T(8,128)} %bitcast.12, s32[16,128]{1,0:T(8,128)} %bitcast.8, s32[16,128]{1,0:T(8,128)} %bitcast.10), custom_call_target="tpu_custom_call" | custom-call | tf_op jit(solution)/shard_map/pallas_call | solution.py:371
  2.2 10.5 %all_to_all.20 = f32[4,160,128]{2,1,0:T(8,128)S(1)} all-to-all(f32[4,160,128]{2,1,0:T(8,128)S(1)} %shard_map.68), channel_id=1, replica_groups=mesh['z'=8,'x'=4,'c'=2,'aa'=8] {'x'}, dimensions={0} | all-to-all | bytes 655360 | tf_op jit(solution)/shard_map/all_to_all | solution.py:381
  12.7 7.6 %all_gather.6.got_ref = f32[8,160,128]{2,1,0:T(8,128)S(1)} all-gather(f32[4,160,128]{2,1,0:T(8,128)S(1)} %all_to_all.20), channel_id=1, replica_groups=mesh['z'=8,'x'=4,'c'=2,'aa'=8] {'c'}, dimensions={0}, use_global_device_ids=true | all-gather | bytes 983040 | tf_op jit(solution)/shard_map/all_gather | solution.py:382
  20.4 13.5 %all_to_all.21.targets_ref.refs_0_ = f32[8,8,128]{2,1,0:T(8,128)S(1)} all-to-all(f32[8,8,128]{2,1,0:T(8,128)S(1)} %get-tuple-element.4), channel_id=1, replica_groups=mesh['z'=8,'x'=4,'c'=2,'aa'=8] {'z'}, dimensions={0} | all-to-all | bytes 65536 | tf_op jit(solution)/shard_map/all_to_all | solution.py:391
  33.9 9.2 %shard_map.70 = f32[8,16,128]{2,1,0:T(8,128)S(1)} custom-call(f32[8,8,128]{2,1,0:T(8,128)S(1)} %all_to_all.21.targets_ref.refs_0_, f32[8,160,128]{2,1,0:T(8,128)S(1)} %all_gather.6.got_ref, f32[16,128]{1,0:T(8,128)S(1)} %get-tuple-element.5.keep_ref), custom_call_target="tpu_custom_call" | custom-call | tf_op jit(solution)/shard_map/pallas_call | solution.py:393
  43.0 9.7 %all_to_all.22.refs_1_ = f32[8,16,128]{2,1,0:T(8,128)S(1)} all-to-all(f32[8,16,128]{2,1,0:T(8,128)S(1)} %shard_map.70), channel_id=1, replica_groups=mesh['z'=8,'x'=4,'c'=2,'aa'=8] {'z'}, dimensions={0} | all-to-all | bytes 131072 | tf_op jit(solution)/shard_map/all_to_all | solution.py:406
  52.7 0.1 shard_map.71
  52.9 17.3 %all_to_all.23 = f32[32,16,128]{2,1,0:T(8,128)S(1)} all-to-all(f32[32,16,128]{2,1,0:T(8,128)S(1)} %shard_map.71), channel_id=1, replica_groups=mesh['z'=8,'x'=4,'c'=2,'aa'=8] {'x','aa'}, dimensions={0} | all-to-all | bytes 524288 | tf_op jit(solution)/shard_map/all_to_all | solution.py:415
  70.2 0.0 copy-start
  70.2 0.0 copy-start.1
  70.2 0.0 copy-start.2
  70.2 0.0 copy-start.3
  70.2 6.3 %all_gather.7 = f32[64,16,128]{2,1,0:T(8,128)S(1)} all-gather(f32[32,16,128]{2,1,0:T(8,128)S(1)} %all_to_all.23), channel_id=1, replica_groups=mesh['z'=8,'x'=4,'c'=2,'aa'=8] {'c'}, dimensions={0}, use_global_device_ids=true | all-gather | bytes 786432 | tf_op jit(solution)/shard_map/all_gather | solution.py:416
  76.4 0.0 copy-done
  76.4 0.0 copy-done.1
  76.4 0.0 copy-done.2
  76.5 0.0 copy-done.3
  76.5 2.3 %shard_map.72 = (f32[12,1280]{1,0:T(8,128)}, f32[12,2048]{1,0:T(8,128)}) custom-call(f32[12,2048]{1,0:T(8,128)S(1)} %copy-done, s32[16,128]{1,0:T(8,128)S(1)} %bitcast.9, s32[16,128]{1,0:T(8,128)S(1)} %bitcast.11, s32[80,128]{1,0:T(8,128)S(1)} %bitcast.7, f32[8,8,16,128]{3,2,1,0:T(8,128)S(1)} %bitcast.5), custom_call_target="tpu_custom_call" | custom-call | tf_op jit(solution)/shard_map/pallas_call | solution.py:418
  (1 shorter events, 0.0 us)
Async XLA Ops:
  70.2 6.3 %copy-start = (f32[12,2048]{1,0:T(8,128)S(1)}, f32[12,2048]{1,0:T(8,128)}, u32[]{:S(2)}) copy-start(f32[12,2048]{1,0:T(8,128)} %state_ref.1) | copy-start | bytes 294916
  70.2 6.3 %copy-start.1 = (s32[10240]{0:T(1024)S(1)}, s32[10240]{0:T(1024)}, u32[]{:S(2)}) copy-start(s32[10240]{0:T(1024)} %param.9) | copy-start | bytes 122884
  70.2 6.3 %copy-start.2 = (s32[2048]{0:T(1024)S(1)}, s32[2048]{0:T(1024)}, u32[]{:S(2)}) copy-start(s32[2048]{0:T(1024)} %param.8) | copy-start | bytes 24580
  70.2 6.3 %copy-start.3 = (s32[2048]{0:T(1024)S(1)}, s32[2048]{0:T(1024)}, u32[]{:S(2)}) copy-start(s32[2048]{0:T(1024)} %param.7) | copy-start | bytes 24580

commit v9 on v8

--- a/solution.py
+++ b/solution.py
@@ -319,16 +319,22 @@
         new_active_ref[6:9, lanes] = tails(c, mine, 3)
         new_active_ref[9:12, lanes] = tails(c, mine, 7)
 
-    row8 = lax.broadcasted_iota(jnp.int32, (8, 128), 0)
+    row16 = lax.broadcasted_iota(jnp.int32, (16, 128), 0)
+    owners = [
+        jnp.where(row16 < edge, float(n), n + 1.0).astype(bf16) for n, edge in enumerate((12, 8, 4))
+    ]
     rows = lax.broadcasted_iota(jnp.int32, (128, 128), 0).astype(f32).astype(bf16)
     nothing, unit = jnp.zeros((16, 128), bf16), jnp.ones((128, 128), bf16)
-    one = jnp.ones((1, 128), f32)
     sums_ref[...] = jnp.zeros_like(sums_ref)
 
     def block(y):
-        tiles = [jnp.where(row8 == 3, 1.0, got_ref[c * X + x, y, 0:8, :]) for c in range(C) for x in range(X)]
+        tiles = [
+            jnp.concatenate([got_ref[c * X + x, y, 0:3, :], got_ref[c * X + x, y, 4:7, :]], axis=0)
+            for c in range(C)
+            for x in range(X)
+        ]
         for c in range(C):
-            tiles.append(jnp.concatenate([tails(c, y, 3), one, tails(c, y, 7), one], axis=0))
+            tiles.append(jnp.concatenate([tails(c, y, 3), tails(c, y, 7)], axis=0))
         lefts, lows = [], []
         for k, tile in enumerate(tiles):
             local = active_ref[pl.ds(y * 10 + k, 1), :] - start
@@ -336,8 +342,17 @@
             low = jnp.broadcast_to(jnp.bitwise_and(local, 127).astype(f32), (128, 128)).astype(bf16)
             lows.append(jnp.where(rows == low, unit, jnp.zeros_like(unit)))
             first = tile.astype(bf16).astype(f32)
-            both = jnp.concatenate([first, tile - first], axis=0).astype(bf16)
-            lefts.append(jnp.concatenate([jnp.where(high == h, both, nothing) for h in range(TILES)], axis=0))
+            both = jnp.concatenate([first, tile - first], axis=0)
+            groups = [
+                jnp.concatenate([both, both[0:4]], axis=0).astype(bf16),
+                jnp.concatenate([both[4:12], both[0:8]], axis=0).astype(bf16),
+                jnp.concatenate([both[8:12], both], axis=0).astype(bf16),
+            ]
+            aims = [high - owner for owner in owners]
+            left = [
+                jnp.where(aim == h, group, nothing) for h in range(0, TILES, 4) for aim, group in zip(aims, groups)
+            ]
+            lefts.append(jnp.concatenate(left, axis=0))
         total = lax.dot_general(
             jnp.concatenate(lefts, axis=1),
             jnp.concatenate(lows, axis=1),
@@ -352,10 +367,12 @@
     for i in range(TILES):
         lanes = slice(i * 128, (i + 1) * 128)
         s = state_ref[:, lanes]
-        forces = sums_ref[i * 16 : i * 16 + 8, :] + sums_ref[i * 16 + 8 : i * 16 + 16, :]
-        acc, jerk, hit = forces[0:3], forces[4:7], forces[3:4] > 0.5
-        dt = ticks_ref[i : i + 1, :].astype(f32) * TICK
-        step = step_of(levels_ref[i : i + 1, :])
+        forces = sums_ref[i * 12 : i * 12 + 6, :] + sums_ref[i * 12 + 6 : i * 12 + 12, :]
+        acc, jerk = forces[0:3], forces[3:6]
+        ticks, levels = ticks_ref[i : i + 1, :], levels_ref[i : i + 1, :]
+        hit = ticks == jnp.left_shift(jnp.ones_like(levels), LEVELS - levels)
+        dt = ticks.astype(f32) * TICK
+        step = step_of(levels)
         pos, vel = predict(s[0:3], s[3:6], s[6:9], s[9:12], dt)
         pos, vel = correct(pos, vel, s[6:9], s[9:12], step, acc, jerk)
         new = jnp.concatenate([pos, vel, acc, jerk], axis=0)
@@ -421,7 +438,7 @@
         in_specs=vmem(5),
         out_specs=vmem(2),
         scratch_shapes=[
-            pltpu.VMEM((256, 128), f32),
+            pltpu.VMEM((192, 128), f32),
         ],
         compiler_params=params(),
     )(state, ticks, levels, active, updates)

time: 79.1 us -> 78.8 us (level)
  no operation moved by 1% of the time
where the time goes in v9:
time: 78.8 us; the launch traced here: 78.5 us
  blocking collectives  64.9 us (82%)
  Pallas kernels  12.9 us (16%)
    all_to_all x1, blocking collectives, per_device(): updates = lax.all_to_all(updates, ('x', 'aa'), 0, 0, tiled=True)  17.3 us
    all_to_all x1, blocking collectives, per_device(): targets = lax.all_to_all(targets, 'z', 0, 0, tiled=True)  13.5 us
    all_to_all x1, blocking collectives, per_device(): got = lax.all_to_all(message, 'x', 0, 0, tiled=True)  10.5 us
    all_to_all x1, blocking collectives, per_device(): partial = lax.all_to_all(partial, 'z', 0, 0, tiled=True)  9.7 us
    pallas_call x1, Pallas kernels, per_device(): pl.pallas_call(force_kernel, out_shape=jax.ShapeDtypeStruct((z_count, 16,...  9.16 us
    all_gather x1, blocking collectives, per_device(): got = lax.all_gather(got, 'c', tiled=True)  7.65 us
    all_gather x1, blocking collectives, per_device(): lax.all_gather(updates, 'c', tiled=True).reshape(GROUPS, y_count, 16, 128)  6.27 us
    pallas_call x1, Pallas kernels, per_device(): pl.pallas_call(store_kernel, out_shape=[jax.ShapeDtypeStruct((12, 1280),...  2.08 us

profile of v9, /device:TPU:1, one launch (start us, length us, event | category | flops | bytes accessed | tf_op | source)
XLA Modules:
  0.0 78.5 jit_solution(4887233083114363851)
XLA Ops:
  0.6 1.6 %shard_map.68 = f32[4,160,128]{2,1,0:T(8,128)S(1)} custom-call(s32[80,128]{1,0:T(8,128)} %bitcast.6, f32[12,2048]{1,0:T(8,128)} %state_ref.1, f32[16,128]{1,0:T(8,128)} %bitcast.12, s32[16,128]{1,0:T(8,128)} %bitcast.8, s32[16,128]{1,0:T(8,128)} %bitcast.10), custom_call_target="tpu_custom_call" | custom-call | tf_op jit(solution)/shard_map/pallas_call | solution.py:388
  2.2 10.5 %all_to_all.20 = f32[4,160,128]{2,1,0:T(8,128)S(1)} all-to-all(f32[4,160,128]{2,1,0:T(8,128)S(1)} %shard_map.68), channel_id=1, replica_groups=mesh['z'=8,'x'=4,'c'=2,'aa'=8] {'x'}, dimensions={0} | all-to-all | bytes 655360 | tf_op jit(solution)/shard_map/all_to_all | solution.py:398
  12.7 7.6 %all_gather.6.got_ref = f32[8,160,128]{2,1,0:T(8,128)S(1)} all-gather(f32[4,160,128]{2,1,0:T(8,128)S(1)} %all_to_all.20), channel_id=1, replica_groups=mesh['z'=8,'x'=4,'c'=2,'aa'=8] {'c'}, dimensions={0}, use_global_device_ids=true | all-gather | bytes 983040 | tf_op jit(solution)/shard_map/all_gather | solution.py:399
  20.4 13.5 %all_to_all.21.targets_ref.refs_0_ = f32[8,8,128]{2,1,0:T(8,128)S(1)} all-to-all(f32[8,8,128]{2,1,0:T(8,128)S(1)} %get-tuple-element.4), channel_id=1, replica_groups=mesh['z'=8,'x'=4,'c'=2,'aa'=8] {'z'}, dimensions={0} | all-to-all | bytes 65536 | tf_op jit(solution)/shard_map/all_to_all | solution.py:408
  33.9 9.2 %shard_map.70 = f32[8,16,128]{2,1,0:T(8,128)S(1)} custom-call(f32[8,8,128]{2,1,0:T(8,128)S(1)} %all_to_all.21.targets_ref.refs_0_, f32[8,160,128]{2,1,0:T(8,128)S(1)} %all_gather.6.got_ref, f32[16,128]{1,0:T(8,128)S(1)} %get-tuple-element.5.keep_ref), custom_call_target="tpu_custom_call" | custom-call | tf_op jit(solution)/shard_map/pallas_call | solution.py:410
  43.0 9.7 %all_to_all.22.refs_1_ = f32[8,16,128]{2,1,0:T(8,128)S(1)} all-to-all(f32[8,16,128]{2,1,0:T(8,128)S(1)} %shard_map.70), channel_id=1, replica_groups=mesh['z'=8,'x'=4,'c'=2,'aa'=8] {'z'}, dimensions={0} | all-to-all | bytes 131072 | tf_op jit(solution)/shard_map/all_to_all | solution.py:423
  52.7 0.1 shard_map.71
  52.9 17.3 %all_to_all.23 = f32[32,16,128]{2,1,0:T(8,128)S(1)} all-to-all(f32[32,16,128]{2,1,0:T(8,128)S(1)} %shard_map.71), channel_id=1, replica_groups=mesh['z'=8,'x'=4,'c'=2,'aa'=8] {'x','aa'}, dimensions={0} | all-to-all | bytes 524288 | tf_op jit(solution)/shard_map/all_to_all | solution.py:432
  70.2 0.0 copy-start
  70.2 0.0 copy-start.1
  70.2 0.0 copy-start.2
  70.2 0.0 copy-start.3
  70.2 6.3 %all_gather.7 = f32[64,16,128]{2,1,0:T(8,128)S(1)} all-gather(f32[32,16,128]{2,1,0:T(8,128)S(1)} %all_to_all.23), channel_id=1, replica_groups=mesh['z'=8,'x'=4,'c'=2,'aa'=8] {'c'}, dimensions={0}, use_global_device_ids=true | all-gather | bytes 786432 | tf_op jit(solution)/shard_map/all_gather | solution.py:433
  76.4 0.0 copy-done
  76.4 0.0 copy-done.1
  76.4 0.0 copy-done.2
  76.5 0.0 copy-done.3
  76.5 2.1 %shard_map.72 = (f32[12,1280]{1,0:T(8,128)}, f32[12,2048]{1,0:T(8,128)}) custom-call(f32[12,2048]{1,0:T(8,128)S(1)} %copy-done, s32[16,128]{1,0:T(8,128)S(1)} %bitcast.9, s32[16,128]{1,0:T(8,128)S(1)} %bitcast.11, s32[80,128]{1,0:T(8,128)S(1)} %bitcast.7, f32[8,8,16,128]{3,2,1,0:T(8,128)S(1)} %bitcast.5), custom_call_target="tpu_custom_call" | custom-call | tf_op jit(solution)/shard_map/pallas_call | solution.py:435
  (1 shorter events, 0.0 us)
Async XLA Ops:
  70.2 6.3 %copy-start = (f32[12,2048]{1,0:T(8,128)S(1)}, f32[12,2048]{1,0:T(8,128)}, u32[]{:S(2)}) copy-start(f32[12,2048]{1,0:T(8,128)} %state_ref.1) | copy-start | bytes 294916
  70.2 6.3 %copy-start.1 = (s32[10240]{0:T(1024)S(1)}, s32[10240]{0:T(1024)}, u32[]{:S(2)}) copy-start(s32[10240]{0:T(1024)} %param.9) | copy-start | bytes 122884
  70.2 6.3 %copy-start.2 = (s32[2048]{0:T(1024)S(1)}, s32[2048]{0:T(1024)}, u32[]{:S(2)}) copy-start(s32[2048]{0:T(1024)} %param.8) | copy-start | bytes 24580
  70.2 6.3 %copy-start.3 = (s32[2048]{0:T(1024)S(1)}, s32[2048]{0:T(1024)}, u32[]{:S(2)}) copy-start(s32[2048]{0:T(1024)} %param.7) | copy-start | bytes 24580

commit v10 on v9

--- a/solution.py
+++ b/solution.py
@@ -116,23 +116,30 @@
         main = picks[g]
         tail = picks[8 + g // 4][:, (g % 4) * TAIL : (g % 4 + 1) * TAIL]
         step = [main[14:15, n * TAIL : (n + 1) * TAIL] for n in range(4)]
-        x, row = g % X, FIELD + 16 * (g // X)
-        for n, q in enumerate((0, 3, 8, 11)):
-            msg_ref[x, row + 4 * n : row + 4 * n + 4, :] = pack(main[q : q + 3], tail[q : q + 3], step[n])
-        msg_ref[x, 8 * (g // X) + 7 : 8 * (g // X) + 8, :] = jnp.concatenate([tail[14:15], jnp.zeros((1, 96), f32)], axis=1)
+        x, c = g % X, g // X
+        packs = [pack(main[q : q + 3], tail[q : q + 3], step[n]) for n, q in enumerate((0, 3, 8, 11))]
+        msg_ref[x, FIELD + 8 * c : FIELD + 8 * c + 4, :] = packs[0]
+        msg_ref[x, FIELD + 8 * c + 4 : FIELD + 8 * c + 8, :] = packs[1]
+        for r in range(8):
+            row = 8 * (8 * c + r) + 7
+            msg_ref[x, row : row + 1, :] = packs[2 + r // 4][r % 4 : r % 4 + 1]
+        row = FIELD + 8 * C + c
+        msg_ref[x, row : row + 1, :] = jnp.concatenate([tail[14:15], jnp.zeros((1, 96), f32)], axis=1)
 
 
 def sum_kernel(got_ref, out_ref, keep_ref):
     c = lax.axis_index("c")
-    picks = pl.ds(pl.multiple_of(FIELD + 16 * c, 16), 16)
-    total = got_ref[0, picks, :]
-    step = got_ref[0, pl.ds(8 * c + 7, 1), :]
+    picks = pl.ds(pl.multiple_of(FIELD + 8 * c, 8), 8)
+    olds = pl.ds(64 * c + 7, 8, stride=8)
+    steps = pl.ds(FIELD + 8 * C + c, 1)
+    total, old, step = got_ref[0, picks, :], got_ref[0, olds, :], got_ref[0, steps, :]
     for g in range(1, GROUPS):
         total = total + got_ref[g, picks, :]
-        step = step + got_ref[g, pl.ds(8 * c + 7, 1), :]
+        old = old + got_ref[g, olds, :]
+        step = step + got_ref[g, steps, :]
     for z in range(out_ref.shape[0]):
-        out_ref[z] = total[0:8]
-    keep_ref[0:8, :] = total[8:16]
+        out_ref[z] = total
+    keep_ref[0:8, :] = old
     keep_ref[8:16, :] = jnp.broadcast_to(step, (8, 128))
 
 
@@ -387,7 +394,7 @@
 
     message = pl.pallas_call(
         pick_kernel,
-        out_shape=jax.ShapeDtypeStruct((X, FIELD + 16 * C, 128), f32),
+        out_shape=jax.ShapeDtypeStruct((X, FIELD + 8 * C + 8, 128), f32),
         in_specs=[pl.BlockSpec(memory_space=pltpu.HBM)] * 5,
         out_specs=vmem(1)[0],
         scratch_shapes=[pltpu.VMEM((384, 256), bf16), pltpu.VMEM((256, 1280), bf16)]

time: 78.8 us -> 78.6 us (level)
  no operation moved by 1% of the time
where the time goes in v10:
time: 78.6 us; the launch traced here: 78.3 us
  blocking collectives  64.7 us (82%)
  Pallas kernels  12.9 us (16%)
    all_to_all x1, blocking collectives, per_device(): updates = lax.all_to_all(updates, ('x', 'aa'), 0, 0, tiled=True)  17.3 us
    all_to_all x1, blocking collectives, per_device(): targets = lax.all_to_all(targets, 'z', 0, 0, tiled=True)  13.4 us
    all_to_all x1, blocking collectives, per_device(): got = lax.all_to_all(message, 'x', 0, 0, tiled=True)  10.4 us
    all_to_all x1, blocking collectives, per_device(): partial = lax.all_to_all(partial, 'z', 0, 0, tiled=True)  9.7 us
    pallas_call x1, Pallas kernels, per_device(): pl.pallas_call(force_kernel, out_shape=jax.ShapeDtypeStruct((z_count, 16,...  9.12 us
    all_gather x1, blocking collectives, per_device(): got = lax.all_gather(got, 'c', tiled=True)  7.62 us
    all_gather x1, blocking collectives, per_device(): lax.all_gather(updates, 'c', tiled=True).reshape(GROUPS, y_count, 16, 128)  6.27 us
    pallas_call x1, Pallas kernels, per_device(): pl.pallas_call(store_kernel, out_shape=[jax.ShapeDtypeStruct((12, 1280),...  2.08 us

profile of v10, /device:TPU:1, one launch (start us, length us, event | category | flops | bytes accessed | tf_op | source)
XLA Modules:
  0.0 78.3 jit_solution(16604466604137353510)
XLA Ops:
  0.6 1.6 %shard_map.68 = f32[4,152,128]{2,1,0:T(8,128)S(1)} custom-call(s32[80,128]{1,0:T(8,128)} %bitcast.6, f32[12,2048]{1,0:T(8,128)} %state_ref.1, f32[16,128]{1,0:T(8,128)} %bitcast.12, s32[16,128]{1,0:T(8,128)} %bitcast.8, s32[16,128]{1,0:T(8,128)} %bitcast.10), custom_call_target="tpu_custom_call" | custom-call | tf_op jit(solution)/shard_map/pallas_call | solution.py:395
  2.2 10.4 %all_to_all.20 = f32[4,152,128]{2,1,0:T(8,128)S(1)} all-to-all(f32[4,152,128]{2,1,0:T(8,128)S(1)} %shard_map.68), channel_id=1, replica_groups=mesh['z'=8,'x'=4,'c'=2,'aa'=8] {'x'}, dimensions={0} | all-to-all | bytes 622592 | tf_op jit(solution)/shard_map/all_to_all | solution.py:405
  12.7 7.6 %all_gather.6.got_ref = f32[8,152,128]{2,1,0:T(8,128)S(1)} all-gather(f32[4,152,128]{2,1,0:T(8,128)S(1)} %all_to_all.20), channel_id=1, replica_groups=mesh['z'=8,'x'=4,'c'=2,'aa'=8] {'c'}, dimensions={0}, use_global_device_ids=true | all-gather | bytes 933888 | tf_op jit(solution)/shard_map/all_gather | solution.py:406
  20.3 13.4 %all_to_all.21.targets_ref.refs_0_ = f32[8,8,128]{2,1,0:T(8,128)S(1)} all-to-all(f32[8,8,128]{2,1,0:T(8,128)S(1)} %get-tuple-element.4), channel_id=1, replica_groups=mesh['z'=8,'x'=4,'c'=2,'aa'=8] {'z'}, dimensions={0} | all-to-all | bytes 65536 | tf_op jit(solution)/shard_map/all_to_all | solution.py:415
  33.7 9.1 %shard_map.70 = f32[8,16,128]{2,1,0:T(8,128)S(1)} custom-call(f32[8,8,128]{2,1,0:T(8,128)S(1)} %all_to_all.21.targets_ref.refs_0_, f32[8,152,128]{2,1,0:T(8,128)S(1)} %all_gather.6.got_ref, f32[16,128]{1,0:T(8,128)S(1)} %get-tuple-element.5.keep_ref), custom_call_target="tpu_custom_call" | custom-call | tf_op jit(solution)/shard_map/pallas_call | solution.py:417
  42.8 9.7 %all_to_all.22.refs_1_ = f32[8,16,128]{2,1,0:T(8,128)S(1)} all-to-all(f32[8,16,128]{2,1,0:T(8,128)S(1)} %shard_map.70), channel_id=1, replica_groups=mesh['z'=8,'x'=4,'c'=2,'aa'=8] {'z'}, dimensions={0} | all-to-all | bytes 131072 | tf_op jit(solution)/shard_map/all_to_all | solution.py:430
  52.5 0.1 shard_map.71
  52.6 17.3 %all_to_all.23 = f32[32,16,128]{2,1,0:T(8,128)S(1)} all-to-all(f32[32,16,128]{2,1,0:T(8,128)S(1)} %shard_map.71), channel_id=1, replica_groups=mesh['z'=8,'x'=4,'c'=2,'aa'=8] {'x','aa'}, dimensions={0} | all-to-all | bytes 524288 | tf_op jit(solution)/shard_map/all_to_all | solution.py:439
  69.9 0.0 copy-start
  69.9 0.0 copy-start.1
  69.9 0.0 copy-start.2
  69.9 0.0 copy-start.3
  69.9 6.3 %all_gather.7 = f32[64,16,128]{2,1,0:T(8,128)S(1)} all-gather(f32[32,16,128]{2,1,0:T(8,128)S(1)} %all_to_all.23), channel_id=1, replica_groups=mesh['z'=8,'x'=4,'c'=2,'aa'=8] {'c'}, dimensions={0}, use_global_device_ids=true | all-gather | bytes 786432 | tf_op jit(solution)/shard_map/all_gather | solution.py:440
  76.2 0.0 copy-done
  76.2 0.0 copy-done.1
  76.2 0.0 copy-done.2
  76.2 0.0 copy-done.3
  76.2 2.1 %shard_map.72 = (f32[12,1280]{1,0:T(8,128)}, f32[12,2048]{1,0:T(8,128)}) custom-call(f32[12,2048]{1,0:T(8,128)S(1)} %copy-done, s32[16,128]{1,0:T(8,128)S(1)} %bitcast.9, s32[16,128]{1,0:T(8,128)S(1)} %bitcast.11, s32[80,128]{1,0:T(8,128)S(1)} %bitcast.7, f32[8,8,16,128]{3,2,1,0:T(8,128)S(1)} %bitcast.5), custom_call_target="tpu_custom_call" | custom-call | tf_op jit(solution)/shard_map/pallas_call | solution.py:442
  (1 shorter events, 0.0 us)
Async XLA Ops:
  69.9 6.3 %copy-start = (f32[12,2048]{1,0:T(8,128)S(1)}, f32[12,2048]{1,0:T(8,128)}, u32[]{:S(2)}) copy-start(f32[12,2048]{1,0:T(8,128)} %state_ref.1) | copy-start | bytes 294916
  69.9 6.3 %copy-start.1 = (s32[10240]{0:T(1024)S(1)}, s32[10240]{0:T(1024)}, u32[]{:S(2)}) copy-start(s32[10240]{0:T(1024)} %param.9) | copy-start | bytes 122884
  69.9 6.3 %copy-start.2 = (s32[2048]{0:T(1024)S(1)}, s32[2048]{0:T(1024)}, u32[]{:S(2)}) copy-start(s32[2048]{0:T(1024)} %param.8) | copy-start | bytes 24580
  69.9 6.3 %copy-start.3 = (s32[2048]{0:T(1024)S(1)}, s32[2048]{0:T(1024)}, u32[]{:S(2)}) copy-start(s32[2048]{0:T(1024)} %param.7) | copy-start | bytes 24580

commit v11 on v10

--- a/solution.py
+++ b/solution.py
@@ -17,7 +17,7 @@
 PER = MAIN + TAIL
 FIELD = 8 * TILES
 CHUNK = 1024
-ROWS = 16
+ROWS = 32
 BLOCKS = PER // ROWS
 CROSSED = MAIN // ROWS
 UNROLL = 8

time: 78.6 us -> 78.6 us (level)
  no operation moved by 1% of the time
where the time goes in v11:
time: 78.6 us; the launch traced here: 78.3 us
  blocking collectives  64.7 us (82%)
  Pallas kernels  12.9 us (16%)
    all_to_all x1, blocking collectives, per_device(): updates = lax.all_to_all(updates, ('x', 'aa'), 0, 0, tiled=True)  17.3 us
    all_to_all x1, blocking collectives, per_device(): targets = lax.all_to_all(targets, 'z', 0, 0, tiled=True)  13.4 us
    all_to_all x1, blocking collectives, per_device(): got = lax.all_to_all(message, 'x', 0, 0, tiled=True)  10.4 us
    all_to_all x1, blocking collectives, per_device(): partial = lax.all_to_all(partial, 'z', 0, 0, tiled=True)  9.7 us
    pallas_call x1, Pallas kernels, per_device(): pl.pallas_call(force_kernel, out_shape=jax.ShapeDtypeStruct((z_count, 16,...  9.16 us
    all_gather x1, blocking collectives, per_device(): got = lax.all_gather(got, 'c', tiled=True)  7.62 us
    all_gather x1, blocking collectives, per_device(): lax.all_gather(updates, 'c', tiled=True).reshape(GROUPS, y_count, 16, 128)  6.27 us
    pallas_call x1, Pallas kernels, per_device(): pl.pallas_call(store_kernel, out_shape=[jax.ShapeDtypeStruct((12, 1280),...  2.08 us

profile of v11, /device:TPU:1, one launch (start us, length us, event | category | flops | bytes accessed | tf_op | source)
XLA Modules:
  0.0 78.3 jit_solution(766363161252142653)
XLA Ops:
  0.6 1.6 %shard_map.68 = f32[4,152,128]{2,1,0:T(8,128)S(1)} custom-call(s32[80,128]{1,0:T(8,128)} %bitcast.6, f32[12,2048]{1,0:T(8,128)} %state_ref.1, f32[16,128]{1,0:T(8,128)} %bitcast.12, s32[16,128]{1,0:T(8,128)} %bitcast.8, s32[16,128]{1,0:T(8,128)} %bitcast.10), custom_call_target="tpu_custom_call" | custom-call | tf_op jit(solution)/shard_map/pallas_call | solution.py:395
  2.2 10.4 %all_to_all.20 = f32[4,152,128]{2,1,0:T(8,128)S(1)} all-to-all(f32[4,152,128]{2,1,0:T(8,128)S(1)} %shard_map.68), channel_id=1, replica_groups=mesh['z'=8,'x'=4,'c'=2,'aa'=8] {'x'}, dimensions={0} | all-to-all | bytes 622592 | tf_op jit(solution)/shard_map/all_to_all | solution.py:405
  12.7 7.6 %all_gather.6.got_ref = f32[8,152,128]{2,1,0:T(8,128)S(1)} all-gather(f32[4,152,128]{2,1,0:T(8,128)S(1)} %all_to_all.20), channel_id=1, replica_groups=mesh['z'=8,'x'=4,'c'=2,'aa'=8] {'c'}, dimensions={0}, use_global_device_ids=true | all-gather | bytes 933888 | tf_op jit(solution)/shard_map/all_gather | solution.py:406
  20.3 13.4 %all_to_all.21.targets_ref.refs_0_ = f32[8,8,128]{2,1,0:T(8,128)S(1)} all-to-all(f32[8,8,128]{2,1,0:T(8,128)S(1)} %get-tuple-element.4), channel_id=1, replica_groups=mesh['z'=8,'x'=4,'c'=2,'aa'=8] {'z'}, dimensions={0} | all-to-all | bytes 65536 | tf_op jit(solution)/shard_map/all_to_all | solution.py:415
  33.7 9.2 %shard_map.70 = f32[8,16,128]{2,1,0:T(8,128)S(1)} custom-call(f32[8,8,128]{2,1,0:T(8,128)S(1)} %all_to_all.21.targets_ref.refs_0_, f32[8,152,128]{2,1,0:T(8,128)S(1)} %all_gather.6.got_ref, f32[16,128]{1,0:T(8,128)S(1)} %get-tuple-element.5.keep_ref), custom_call_target="tpu_custom_call" | custom-call | tf_op jit(solution)/shard_map/pallas_call | solution.py:417
  42.8 9.7 %all_to_all.22.refs_1_ = f32[8,16,128]{2,1,0:T(8,128)S(1)} all-to-all(f32[8,16,128]{2,1,0:T(8,128)S(1)} %shard_map.70), channel_id=1, replica_groups=mesh['z'=8,'x'=4,'c'=2,'aa'=8] {'z'}, dimensions={0} | all-to-all | bytes 131072 | tf_op jit(solution)/shard_map/all_to_all | solution.py:430
  52.5 0.1 shard_map.71
  52.7 17.3 %all_to_all.23 = f32[32,16,128]{2,1,0:T(8,128)S(1)} all-to-all(f32[32,16,128]{2,1,0:T(8,128)S(1)} %shard_map.71), channel_id=1, replica_groups=mesh['z'=8,'x'=4,'c'=2,'aa'=8] {'x','aa'}, dimensions={0} | all-to-all | bytes 524288 | tf_op jit(solution)/shard_map/all_to_all | solution.py:439
  70.0 0.0 copy-start
  70.0 0.0 copy-start.1
  70.0 0.0 copy-start.2
  70.0 0.0 copy-start.3
  70.0 6.3 %all_gather.7 = f32[64,16,128]{2,1,0:T(8,128)S(1)} all-gather(f32[32,16,128]{2,1,0:T(8,128)S(1)} %all_to_all.23), channel_id=1, replica_groups=mesh['z'=8,'x'=4,'c'=2,'aa'=8] {'c'}, dimensions={0}, use_global_device_ids=true | all-gather | bytes 786432 | tf_op jit(solution)/shard_map/all_gather | solution.py:440
  76.2 0.0 copy-done
  76.2 0.0 copy-done.1
  76.3 0.0 copy-done.2
  76.3 0.0 copy-done.3
  76.3 2.1 %shard_map.72 = (f32[12,1280]{1,0:T(8,128)}, f32[12,2048]{1,0:T(8,128)}) custom-call(f32[12,2048]{1,0:T(8,128)S(1)} %copy-done, s32[16,128]{1,0:T(8,128)S(1)} %bitcast.9, s32[16,128]{1,0:T(8,128)S(1)} %bitcast.11, s32[80,128]{1,0:T(8,128)S(1)} %bitcast.7, f32[8,8,16,128]{3,2,1,0:T(8,128)S(1)} %bitcast.5), custom_call_target="tpu_custom_call" | custom-call | tf_op jit(solution)/shard_map/pallas_call | solution.py:442
  (1 shorter events, 0.0 us)
Async XLA Ops:
  70.0 6.3 %copy-start = (f32[12,2048]{1,0:T(8,128)S(1)}, f32[12,2048]{1,0:T(8,128)}, u32[]{:S(2)}) copy-start(f32[12,2048]{1,0:T(8,128)} %state_ref.1) | copy-start | bytes 294916
  70.0 6.3 %copy-start.1 = (s32[10240]{0:T(1024)S(1)}, s32[10240]{0:T(1024)}, u32[]{:S(2)}) copy-start(s32[10240]{0:T(1024)} %param.9) | copy-start | bytes 122884
  70.0 6.3 %copy-start.2 = (s32[2048]{0:T(1024)S(1)}, s32[2048]{0:T(1024)}, u32[]{:S(2)}) copy-start(s32[2048]{0:T(1024)} %param.8) | copy-start | bytes 24580
  70.0 6.3 %copy-start.3 = (s32[2048]{0:T(1024)S(1)}, s32[2048]{0:T(1024)}, u32[]{:S(2)}) copy-start(s32[2048]{0:T(1024)} %param.7) | copy-start | bytes 24580

commit v12 on v10

--- a/solution.py
+++ b/solution.py
@@ -138,9 +138,9 @@
         old = old + got_ref[g, olds, :]
         step = step + got_ref[g, steps, :]
     for z in range(out_ref.shape[0]):
-        out_ref[z] = total
-    keep_ref[0:8, :] = old
-    keep_ref[8:16, :] = jnp.broadcast_to(step, (8, 128))
+        out_ref[z, 0:8, :] = total
+        out_ref[z, 8:16, :] = old
+    keep_ref[...] = jnp.broadcast_to(step, (8, 128))
 
 
 def weight_rows(tile, row, center):
@@ -173,9 +173,9 @@
 
 
 def force_kernel(targets_ref, got_ref, keep_ref, out_ref, seen_ref, left_ref, along_ref, sums_ref):
-    target = targets_ref[0]
+    target = targets_ref[0, 0:8, :]
     for z in range(1, targets_ref.shape[0]):
-        target = target + targets_ref[z]
+        target = target + targets_ref[z, 0:8, :]
     columns = jnp.transpose(target)
     for q in range(3):
         seen_ref[q, 0:MAIN, :] = jnp.broadcast_to(columns[:, q : q + 1], (MAIN, 128))
@@ -277,11 +277,10 @@
     vel = target[4:8] - pack(center[3:6], center[3:6, 0:TAIL])
     acc = cube_pos - pos * cube_one
     jerk = (cube_vel - vel * cube_one) - 3.0 * (rate_pos - pos * rate_one)
-    last = jnp.concatenate([acc[3:4, 0:96], keep_ref[8:9, 0:TAIL]], axis=1)
+    last = jnp.concatenate([acc[3:4, 0:96], keep_ref[0:1, 0:TAIL]], axis=1)
     forces = jnp.concatenate([acc[0:3], last, jerk], axis=0)
     for z in range(out_ref.shape[0]):
-        out_ref[z, 0:8, :] = forces
-        out_ref[z, 8:16, :] = keep_ref[0:8, :]
+        out_ref[z] = forces
 
 
 def correct_kernel(scale, targets_ref, got_ref, out_ref):
@@ -290,9 +289,9 @@
     for z in range(1, targets_ref.shape[0]):
         target = target + targets_ref[z]
         total = total + got_ref[z]
-    forces = total[0:8] * scale
-    old = total[8:16]
-    main = jnp.concatenate([a[r : r + 1, 96:128] for a in (target, old) for r in (3, 7)], axis=1)
+    forces = total * scale
+    old = target[8:16]
+    main = jnp.concatenate([a[r : r + 1, 96:128] for a in (target[0:8], old) for r in (3, 7)], axis=1)
     tail = total[3:4, 96:128]
     step = pack(jnp.concatenate([main, main, main], axis=0), jnp.concatenate([tail, tail, tail], axis=0))
     pos, vel = correct(target[0:4], target[4:8], old[0:4], old[4:8], step, forces[0:4], forces[4:8])
@@ -407,7 +406,7 @@
 
     targets, keep = pl.pallas_call(
         sum_kernel,
-        out_shape=[jax.ShapeDtypeStruct((z_count, 8, 128), f32), jax.ShapeDtypeStruct((16, 128), f32)],
+        out_shape=[jax.ShapeDtypeStruct((z_count, 16, 128), f32), jax.ShapeDtypeStruct((8, 128), f32)],
         in_specs=vmem(1),
         out_specs=vmem(2),
         compiler_params=params(),
@@ -416,7 +415,7 @@
 
     partial = pl.pallas_call(
         force_kernel,
-        out_shape=jax.ShapeDtypeStruct((z_count, 16, 128), f32),
+        out_shape=jax.ShapeDtypeStruct((z_count, 8, 128), f32),
         in_specs=vmem(3),
         out_specs=vmem(1)[0],
         scratch_shapes=[

time: 78.6 us -> 78.6 us (level)
  no operation moved by 1% of the time
where the time goes in v12:
time: 78.6 us; the launch traced here: 78.3 us
  blocking collectives  64.7 us (82%)
  Pallas kernels  12.9 us (16%)
    all_to_all x1, blocking collectives, per_device(): updates = lax.all_to_all(updates, ('x', 'aa'), 0, 0, tiled=True)  17.4 us
    all_to_all x1, blocking collectives, per_device(): targets = lax.all_to_all(targets, 'z', 0, 0, tiled=True)  13.7 us
    all_to_all x1, blocking collectives, per_device(): got = lax.all_to_all(message, 'x', 0, 0, tiled=True)  10.4 us
    all_to_all x1, blocking collectives, per_device(): partial = lax.all_to_all(partial, 'z', 0, 0, tiled=True)  9.25 us
    pallas_call x1, Pallas kernels, per_device(): pl.pallas_call(force_kernel, out_shape=jax.ShapeDtypeStruct((z_count, 8,...  9.11 us
    all_gather x1, blocking collectives, per_device(): got = lax.all_gather(got, 'c', tiled=True)  7.62 us
    all_gather x1, blocking collectives, per_device(): lax.all_gather(updates, 'c', tiled=True).reshape(GROUPS, y_count, 16, 128)  6.33 us
    pallas_call x1, Pallas kernels, per_device(): pl.pallas_call(store_kernel, out_shape=[jax.ShapeDtypeStruct((12, 1280),...  2.08 us

profile of v12, /device:TPU:1, one launch (start us, length us, event | category | flops | bytes accessed | tf_op | source)
XLA Modules:
  0.0 78.3 jit_solution(11261765664576275075)
XLA Ops:
  0.6 1.6 %shard_map.68 = f32[4,152,128]{2,1,0:T(8,128)S(1)} custom-call(s32[80,128]{1,0:T(8,128)} %bitcast.6, f32[12,2048]{1,0:T(8,128)} %state_ref.1, f32[16,128]{1,0:T(8,128)} %bitcast.12, s32[16,128]{1,0:T(8,128)} %bitcast.8, s32[16,128]{1,0:T(8,128)} %bitcast.10), custom_call_target="tpu_custom_call" | custom-call | tf_op jit(solution)/shard_map/pallas_call | solution.py:394
  2.2 10.4 %all_to_all.20 = f32[4,152,128]{2,1,0:T(8,128)S(1)} all-to-all(f32[4,152,128]{2,1,0:T(8,128)S(1)} %shard_map.68), channel_id=1, replica_groups=mesh['z'=8,'x'=4,'c'=2,'aa'=8] {'x'}, dimensions={0} | all-to-all | bytes 622592 | tf_op jit(solution)/shard_map/all_to_all | solution.py:404
  12.7 7.6 %all_gather.6.got_ref = f32[8,152,128]{2,1,0:T(8,128)S(1)} all-gather(f32[4,152,128]{2,1,0:T(8,128)S(1)} %all_to_all.20), channel_id=1, replica_groups=mesh['z'=8,'x'=4,'c'=2,'aa'=8] {'c'}, dimensions={0}, use_global_device_ids=true | all-gather | bytes 933888 | tf_op jit(solution)/shard_map/all_gather | solution.py:405
  20.3 13.7 %all_to_all.21.targets_ref.refs_0_ = f32[8,16,128]{2,1,0:T(8,128)S(1)} all-to-all(f32[8,16,128]{2,1,0:T(8,128)S(1)} %get-tuple-element.4), channel_id=1, replica_groups=mesh['z'=8,'x'=4,'c'=2,'aa'=8] {'z'}, dimensions={0} | all-to-all | bytes 131072 | tf_op jit(solution)/shard_map/all_to_all | solution.py:414
  34.0 9.1 %shard_map.70 = f32[8,8,128]{2,1,0:T(8,128)S(1)} custom-call(f32[8,16,128]{2,1,0:T(8,128)S(1)} %all_to_all.21.targets_ref.refs_0_, f32[8,152,128]{2,1,0:T(8,128)S(1)} %all_gather.6.got_ref, f32[8,128]{1,0:T(8,128)S(1)} %get-tuple-element.5.keep_ref), custom_call_target="tpu_custom_call" | custom-call | tf_op jit(solution)/shard_map/pallas_call | solution.py:416
  43.1 9.2 %all_to_all.22.refs_1_ = f32[8,8,128]{2,1,0:T(8,128)S(1)} all-to-all(f32[8,8,128]{2,1,0:T(8,128)S(1)} %shard_map.70), channel_id=1, replica_groups=mesh['z'=8,'x'=4,'c'=2,'aa'=8] {'z'}, dimensions={0} | all-to-all | bytes 65536 | tf_op jit(solution)/shard_map/all_to_all | solution.py:429
  52.3 0.1 shard_map.71
  52.4 17.4 %all_to_all.23 = f32[32,16,128]{2,1,0:T(8,128)S(1)} all-to-all(f32[32,16,128]{2,1,0:T(8,128)S(1)} %shard_map.71), channel_id=1, replica_groups=mesh['z'=8,'x'=4,'c'=2,'aa'=8] {'x','aa'}, dimensions={0} | all-to-all | bytes 524288 | tf_op jit(solution)/shard_map/all_to_all | solution.py:438
  69.9 0.0 copy-start
  69.9 0.0 copy-start.1
  69.9 0.0 copy-start.2
  69.9 0.0 copy-start.3
  69.9 6.3 %all_gather.7 = f32[64,16,128]{2,1,0:T(8,128)S(1)} all-gather(f32[32,16,128]{2,1,0:T(8,128)S(1)} %all_to_all.23), channel_id=1, replica_groups=mesh['z'=8,'x'=4,'c'=2,'aa'=8] {'c'}, dimensions={0}, use_global_device_ids=true | all-gather | bytes 786432 | tf_op jit(solution)/shard_map/all_gather | solution.py:439
  76.2 0.0 copy-done
  76.2 0.0 copy-done.1
  76.2 0.0 copy-done.2
  76.2 0.0 copy-done.3
  76.2 2.1 %shard_map.72 = (f32[12,1280]{1,0:T(8,128)}, f32[12,2048]{1,0:T(8,128)}) custom-call(f32[12,2048]{1,0:T(8,128)S(1)} %copy-done, s32[16,128]{1,0:T(8,128)S(1)} %bitcast.9, s32[16,128]{1,0:T(8,128)S(1)} %bitcast.11, s32[80,128]{1,0:T(8,128)S(1)} %bitcast.7, f32[8,8,16,128]{3,2,1,0:T(8,128)S(1)} %bitcast.5), custom_call_target="tpu_custom_call" | custom-call | tf_op jit(solution)/shard_map/pallas_call | solution.py:441
  (1 shorter events, 0.0 us)
Async XLA Ops:
  69.9 6.3 %copy-start = (f32[12,2048]{1,0:T(8,128)S(1)}, f32[12,2048]{1,0:T(8,128)}, u32[]{:S(2)}) copy-start(f32[12,2048]{1,0:T(8,128)} %state_ref.1) | copy-start | bytes 294916
  69.9 6.3 %copy-start.1 = (s32[10240]{0:T(1024)S(1)}, s32[10240]{0:T(1024)}, u32[]{:S(2)}) copy-start(s32[10240]{0:T(1024)} %param.9) | copy-start | bytes 122884
  69.9 6.3 %copy-start.2 = (s32[2048]{0:T(1024)S(1)}, s32[2048]{0:T(1024)}, u32[]{:S(2)}) copy-start(s32[2048]{0:T(1024)} %param.8) | copy-start | bytes 24580
  69.9 6.3 %copy-start.3 = (s32[2048]{0:T(1024)S(1)}, s32[2048]{0:T(1024)}, u32[]{:S(2)}) copy-start(s32[2048]{0:T(1024)} %param.7) | copy-start | bytes 24580
